TPU v7x, 256 devices: a whole 4x4x8 slice. The times are simulated.
256 devices in a mesh: replica: 16 (over z_hi, x), fsdp: 16 (over z_lo, y, core).
Axes of the slice: x: 4, y: 4, z: 8 (z_hi: 4, z_lo: 2; z = z_hi * 2 + z_lo), core: 2. Of those that a mesh axis runs over, the one named last changes fastest.
Arguments:
- inputs: bfloat16 [16, 3072, 8192], P('replica', 'fsdp'), may hold values from -6 to 6
- out_grad: bfloat16 [16, 3072, 8192], P('replica', 'fsdp'), may hold values from -6 to 6
- queries: bfloat16 [16, 3072, 256], P('replica', 'fsdp'), may hold values from -5.5 to 5.5
- key_states: bfloat16 [16, 3072, 128], P('replica', 'fsdp'), may hold values from -5.5 to 5.5
- value_states: bfloat16 [16, 3072, 128], P('replica', 'fsdp'), may hold values from -6 to 6
- weights: bfloat16 [16, 8192, 768], P('replica', 'fsdp'), may hold values from -0.0625 to 0.0625
- frag_delta: float32 [16, 8192, 128], P('replica', 'fsdp'), may hold values from -6 to 6
- frag_params: float32 [8192, 128], P('fsdp'), may hold values from -6 to 6
- frag_moment: float32 [8192, 128], P('fsdp'), may hold values from -3 to 3
Outputs:
- input_grad: bfloat16 [16, 3072, 8192], P('replica', 'fsdp')
- weight_grad: bfloat16 [16, 8192, 768], P('replica', 'fsdp')
- new_params: float32 [8192, 128], P('fsdp')
- new_moment: float32 [8192, 128], P('fsdp')
All inputs are finite; a program needn't handle non-finite values.
Results may differ from a plain program's by a relative error of at most 0.027.
Values may be sent and summed in bfloat16 or wider, within the bound.
A program may use at most 128 MiB of HBM per device.

v0:
```python
import math

import jax
import jax.numpy as jnp
from jax import lax
from jax.sharding import PartitionSpec as P

rope_base = 500000.0
outer_rate = 0.7
outer_beta = 0.9
masked_score = -1e30


def rotate_back(gradient, positions):
    head_dim = gradient.shape[-1]
    half_dim = head_dim // 2
    inverse_freq = jnp.exp(
        -math.log(rope_base) * 2.0 * jnp.arange(half_dim, dtype=jnp.float32) / head_dim
    )
    angles = positions.astype(jnp.float32)[:, None] * inverse_freq[None, :]
    cosine_part = jnp.cos(angles)[:, None, :]
    sine_part = jnp.sin(angles)[:, None, :]
    low_half = gradient[..., :half_dim]
    high_half = gradient[..., half_dim:]
    return jnp.concatenate(
        [
            low_half * cosine_part + high_half * sine_part,
            high_half * cosine_part - low_half * sine_part,
        ],
        axis=-1,
    )


def body(
    inputs,
    out_grad,
    queries,
    key_states,
    value_states,
    weights,
    frag_delta,
    frag_params,
    frag_moment,
):
    replicas = lax.axis_size("replica")
    summed = lax.psum(frag_delta[0].astype(jnp.bfloat16), "replica").astype(jnp.float32)
    outer_grad = summed / replicas
    moment_next = outer_beta * frag_moment + outer_grad
    params_next = frag_params - outer_rate * (outer_grad + outer_beta * moment_next)
    tokens_dev = inputs.shape[1]
    fsdp_count = lax.axis_size("fsdp")
    seq_len = tokens_dev * fsdp_count
    head_dim = key_states.shape[2]
    head_count = queries.shape[2] // head_dim
    width_qkv = (head_count + 2) * head_dim
    activations = inputs[0]
    grad_rows = out_grad[0]
    own_queries = queries[0].reshape(tokens_dev, head_count, head_dim)
    full_weights = lax.all_gather(weights[0], "fsdp", axis=0, tiled=True)
    attn_grad = jnp.dot(grad_rows, full_weights[:, width_qkv:], preferred_element_type=jnp.float32)
    attn_grad = attn_grad.astype(jnp.bfloat16).reshape(tokens_dev, head_count, head_dim)
    all_keys, all_values = (
        lax.all_gather(key_states[0], "fsdp", axis=0, tiled=True),
        lax.all_gather(value_states[0], "fsdp", axis=0, tiled=True),
    )
    first_token = lax.axis_index("fsdp") * tokens_dev
    query_pos = first_token + jnp.arange(tokens_dev, dtype=jnp.int32)
    key_pos = jnp.arange(seq_len, dtype=jnp.int32)
    visible = key_pos[None, :] <= query_pos[:, None]
    score_scale = 1.0 / math.sqrt(head_dim)
    scores = (
        jnp.einsum("thd,kd->htk", own_queries, all_keys, preferred_element_type=jnp.float32)
        * score_scale
    )
    scores = jnp.where(visible[None], scores, masked_score)
    row_peak = jnp.max(scores, axis=-1, keepdims=True)
    exponent = jnp.exp(scores - row_peak)
    attn_probs = exponent / jnp.sum(exponent, axis=-1, keepdims=True)
    probs_low = attn_probs.astype(jnp.bfloat16)
    attended = jnp.einsum("htk,kd->thd", probs_low, all_values, preferred_element_type=jnp.float32)
    attended = attended.astype(jnp.bfloat16).reshape(tokens_dev, head_count * head_dim)
    prob_grad = jnp.einsum("thd,kd->htk", attn_grad, all_values, preferred_element_type=jnp.float32)
    row_delta = jnp.sum(attn_probs * prob_grad, axis=-1, keepdims=True)
    score_grad = (attn_probs * (prob_grad - row_delta) * score_scale).astype(jnp.bfloat16)
    query_grad = jnp.einsum("htk,kd->thd", score_grad, all_keys, preferred_element_type=jnp.float32)
    key_term = jnp.einsum(
        "htk,thd->kd", score_grad, own_queries, preferred_element_type=jnp.float32
    )
    value_term = jnp.einsum("htk,thd->kd", probs_low, attn_grad, preferred_element_type=jnp.float32)
    key_grad, value_grad = (
        lax.psum_scatter(
            key_term.astype(jnp.bfloat16), "fsdp", scatter_dimension=0, tiled=True
        ).astype(jnp.float32),
        lax.psum_scatter(
            value_term.astype(jnp.bfloat16), "fsdp", scatter_dimension=0, tiled=True
        ).astype(jnp.float32),
    )
    query_grad = (
        rotate_back(query_grad, query_pos)
        .astype(jnp.bfloat16)
        .reshape(tokens_dev, head_count * head_dim)
    )
    key_grad = rotate_back(key_grad[:, None, :], query_pos)[:, 0, :].astype(jnp.bfloat16)
    value_grad = value_grad.astype(jnp.bfloat16)
    proj_grad = jnp.concatenate([query_grad, key_grad, value_grad], axis=1)
    input_grad = lax.dot_general(
        proj_grad,
        full_weights[:, :width_qkv],
        (((1,), (1,)), ((), ())),
        preferred_element_type=jnp.float32,
    )
    input_grad = input_grad.astype(jnp.bfloat16)
    qkv_term = lax.dot_general(
        activations, proj_grad, (((0,), (0,)), ((), ())), preferred_element_type=jnp.float32
    )
    out_term = lax.dot_general(
        grad_rows, attended, (((0,), (0,)), ((), ())), preferred_element_type=jnp.float32
    )
    weight_grad = lax.psum_scatter(
        jnp.concatenate([qkv_term, out_term], axis=1).astype(jnp.bfloat16),
        "fsdp",
        scatter_dimension=0,
        tiled=True,
    )
    return (input_grad[None], weight_grad[None], params_next, moment_next)


def solution(mesh):
    placed = (
        P("replica", "fsdp", None),
        P("replica", "fsdp", None),
        P("replica", "fsdp", None),
        P("replica", "fsdp", None),
        P("replica", "fsdp", None),
        P("replica", "fsdp", None),
        P("replica", "fsdp", None),
        P("fsdp", None),
        P("fsdp", None),
    )
    return jax.shard_map(
        body,
        mesh=mesh,
        in_specs=placed,
        out_specs=(
            P("replica", "fsdp", None),
            P("replica", "fsdp", None),
            P("fsdp", None),
            P("fsdp", None),
        ),
        check_vma=False,
    )
```

profile of v0, /device:TPU:1, one launch (start us, length us, event | category | flops | bytes accessed | tf_op | source)
XLA Modules:
  0.0 342.3 jit_solution(8217087961831487029)
XLA Ops:
  8.1 0.7 all-gather.5.cloned.1.call-update
  8.8 1.1 reshape_squeeze.3
  9.9 27.2 %all-gather = bf16[1,3072,128]{2,1,0:T(8,128)(2,1)} all-gather(bf16[1,192,128]{2,1,0:T(8,128)(2,1)} %param.12), channel_id=2, replica_groups=mesh['replica'=16,'fsdp'=16] {'fsdp'}, dimensions={1}, use_global_device_ids=true | all-gather | bytes 835584 | tf_op jit(solution)/shard_map/all_gather | solution.py:63
  37.1 24.6 %all-gather.2 = bf16[1,3072,128]{2,1,0:T(8,128)(2,1)} all-gather(bf16[1,192,128]{2,1,0:T(8,128)(2,1)} %param.13), channel_id=4, replica_groups=mesh['replica'=16,'fsdp'=16] {'fsdp'}, dimensions={1}, use_global_device_ids=true | all-gather | bytes 835584 | tf_op jit(solution)/shard_map/all_gather | solution.py:64
  61.7 1.2 iota_compare_fusion
  62.9 5.3 %fusion.79 = (f32[2,192]{1,0:T(2,128)S(1)}, f32[2,192,3072]{2,1,0:T(8,128)}) fusion(pred[192,3072]{1,0:T(8,128)(4,1)} %iota_compare_fusion, bf16[1,3072,128]{2,1,0:T(8,128)(2,1)} %all-gather, bf16[192,2,128]{2,1,0:T(2,128)(2,1)S(1)} %reshape_squeeze.3), kind=kOutput, calls=%fused_computation.88 | convolution fusion | flops 306711552 | bytes 6194688 | tf_op jit(solution)/shard_map/sub | solution.py:77
  68.2 24.4 %all-gather.5.cloned.1.call-done = bf16[1,8192,768]{2,1,0:T(8,128)(2,1)} async-done(((bf16[1,512,768]{2,1,0:T(8,128)(2,1)}), bf16[1,8192,768]{2,1,0:T(8,128)(2,1)}) %all-gather.5.cloned.1.call-update) | async-done | bytes 12582928 | tf_op jit(solution)/shard_map/all_gather | solution.py:59
  92.6 4.2 %fusion.35 = bf16[24,2,8,128]{3,2,1,0:T(8,128)(2,1)S(1)} fusion(bf16[8192,768]{1,0:T(8,128)(2,1)} %bitcast.106, bf16[1,192,8192]{2,1,0:T(8,128)(2,1)} %param.10), kind=kOutput, calls=%fused_computation.38 | convolution fusion | flops 805355520 | bytes 7438336 | tf_op jit(solution)/shard_map/dot_general | solution.py:60
  96.8 2.9 fusion.41
  99.7 8.7 %fusion.13 = bf16[3072,128]{1,0:T(8,128)(2,1)} fusion(f32[192,2,3072]{2,0,1:T(8,128)} %fusion.41, bf16[192,2,128]{2,1,0:T(2,128)(2,1)S(1)} %reshape_squeeze.3, f32[2,192,3072]{2,1,0:T(8,128)} %get-tuple-element.21, f32[2,192]{1,0:T(2,128)S(1)} %get-tuple-element.20), kind=kOutput, calls=%fused_computation.22 | convolution fusion | flops 310644096 | bytes 10323456 | tf_op jit(solution)/shard_map/htk,thd->kd/dot_general | solution.py:86
  108.5 4.2 %fusion.14 = bf16[3072,128]{1,0:T(8,128)(2,1)} fusion(bf16[24,2,8,128]{3,2,1,0:T(8,128)(2,1)S(1)} %fusion.35, f32[2,192,3072]{2,1,0:T(8,128)} %get-tuple-element.21, f32[2,192]{1,0:T(2,128)S(1)} %get-tuple-element.20), kind=kOutput, calls=%fused_computation.23 | convolution fusion | flops 304742400 | bytes 5604864 | tf_op jit(solution)/shard_map/htk,thd->kd/dot_general | solution.py:89
  113.8 3.5 %fusion.32 = bf16[2,24,8,128]{3,2,1,0:T(8,128)(2,1)S(1)} fusion(bf16[1,3072,128]{2,1,0:T(8,128)(2,1)} %all-gather.2, f32[2,192,3072]{2,1,0:T(8,128)} %get-tuple-element.21, f32[2,192]{1,0:T(2,128)S(1)} %get-tuple-element.20), kind=kOutput, calls=%fused_computation.37 | convolution fusion | flops 304398336 | bytes 5604864 | tf_op jit(solution)/shard_map/htk,kd->thd/dot_general | solution.py:80
  117.3 3.3 fusion.3
  121.1 7.7 %fusion.23 = f32[192,2,128]{2,0,1:T(8,128)S(1)} fusion(f32[192,2,3072]{2,0,1:T(8,128)} %fusion.41, bf16[1,3072,128]{2,1,0:T(8,128)(2,1)} %all-gather, f32[2,192,3072]{2,1,0:T(8,128)} %get-tuple-element.21, f32[2,192]{1,0:T(2,128)S(1)} %get-tuple-element.20), kind=kOutput, calls=%fused_computation.34 | convolution fusion | flops 310250880 | bytes 10421760 | tf_op jit(solution)/shard_map/htk,kd->thd/dot_general | solution.py:85
  129.0 42.8 %reduce-scatter.4.cloned.1.call-done = bf16[192,128]{1,0:T(8,128)(2,1)} async-done(((bf16[3072,128]{1,0:T(8,128)(2,1)}), bf16[192,128]{1,0:T(8,128)(2,1)}) %reduce-scatter.4.cloned.1.call-update) | async-done | bytes 49168 | tf_op jit(solution)/shard_map/reduce_scatter | solution.py:91
  171.8 0.8 bitcast_convert_fusion
  173.1 64.2 %reduce-scatter.6.cloned.1.call-done = bf16[192,128]{1,0:T(8,128)(2,1)} async-done(((bf16[3072,128]{1,0:T(8,128)(2,1)}), bf16[192,128]{1,0:T(8,128)(2,1)}) %reduce-scatter.6.cloned.1.call-update) | async-done | bytes 49168 | tf_op jit(solution)/shard_map/reduce_scatter | solution.py:94
  237.3 3.3 fusion.2
  240.6 8.6 %pad_maximum_fusion = bf16[8192,768]{0,1:T(8,128)(2,1)} fusion(bf16[8192,256]{0,1:T(8,128)(2,1)S(1)} %copy-done.1, bf16[8192,512]{0,1:T(8,128)(2,1)S(1)} %fusion.2), kind=kLoop, calls=%fused_computation.2 | loop fusion | flops 25165824 | bytes 25165824 | tf_op jit(solution)/shard_map/concatenate | solution.py:120
  249.3 22.3 %all-reduce.2.cloned.1.call-done = bf16[512,128]{1,0:T(8,128)(2,1)} async-done(((bf16[512,128]{1,0:T(8,128)(2,1)}), bf16[512,128]{1,0:T(8,128)(2,1)}) %all-reduce.2.cloned.1.call-update) | async-done | bytes 131088 | tf_op jit(solution)/shard_map/psum | solution.py:46
  271.5 1.9 multiply_subtract_fusion
  273.4 8.1 %fusion.4 = bf16[1,192,8192]{2,1,0:T(8,128)(2,1)} fusion(bf16[8192,768]{1,0:T(8,128)(2,1)} %bitcast.107, bf16[192,128]{1,0:T(8,128)(2,1)} %reduce-scatter.6.cloned.1.call-done, bf16[192,128]{1,0:T(8,128)(2,1)S(1)} %maximum_bitcast_fusion.1, bf16[192,256]{1,0:T(8,128)(2,1)S(1)} %copy_bitcast_fusion), kind=kOutput, calls=%fused_computation.8 | convolution fusion | flops 1612775424 | bytes 11730944 | tf_op jit(solution)/shard_map/dot_general | solution.py:106
  281.5 51.3 %reduce-scatter.8.cloned.1.call-done = bf16[512,768]{0,1:T(8,128)(2,1)} async-done(((bf16[8192,768]{0,1:T(8,128)(2,1)}), bf16[512,768]{0,1:T(8,128)(2,1)}) %reduce-scatter.8.cloned.1.call-update) | async-done | bytes 786448 | tf_op jit(solution)/shard_map/reduce_scatter | solution.py:119
  332.8 2.3 copy.24
  (30 shorter events, 2.4 us)
Async XLA Ops:
  8.0 229.3 %copy-start = (bf16[1,192,8192]{2,1,0:T(8,128)(2,1)S(1)}, bf16[1,192,8192]{2,1,0:T(8,128)(2,1)}, u32[]{:S(2)}) copy-start(bf16[1,192,8192]{2,1,0:T(8,128)(2,1)} %param.9) | copy-start | bytes 9437188
  8.0 84.6 %all-gather.5.cloned.1.call-start = ((), (), s32[]{:S(2)}) async-start(), calls=%async_computation.7 | async-start | bytes 13369344 | tf_op jit(solution)/shard_map/all_gather | solution.py:59
  8.7 163.0 %reduce-scatter.4.cloned.1.call-start = ((), (), s32[]{:S(2)}) async-start(), calls=%async_computation.3 | async-start | bytes 835584 | tf_op jit(solution)/shard_map/reduce_scatter | solution.py:91
  92.6 4.2 %copy-start.3 = (bf16[1,3072,128]{2,1,0:T(8,128)(2,1)S(1)}, bf16[1,3072,128]{2,1,0:T(8,128)(2,1)}, u32[]{:S(2)}) copy-start(bf16[1,3072,128]{2,1,0:T(8,128)(2,1)} %all-gather.2) | copy-start | bytes 2359300
  108.4 4.4 %copy-start.4 = (f32[1,512,128]{2,1,0:T(8,128)S(1)}, f32[1,512,128]{2,1,0:T(8,128)}, u32[]{:S(2)}) copy-start(f32[1,512,128]{2,1,0:T(8,128)} %param.15) | copy-start | bytes 786436
  108.5 128.8 %reduce-scatter.6.cloned.1.call-start = ((), (), s32[]{:S(2)}) async-start(), calls=%async_computation.4 | async-start | bytes 835584 | tf_op jit(solution)/shard_map/reduce_scatter | solution.py:94
  112.7 158.8 %all-reduce.2.cloned.1.call-start = ((), (), s32[]{:S(2)}) async-start(), calls=%async_computation.6 | async-start | bytes 262144 | tf_op jit(solution)/shard_map/psum | solution.py:46
  113.5 219.3 %reduce-scatter.8.cloned.1.call-start = ((), (), s32[]{:S(2)}) async-start(), calls=%async_computation.5 | async-start | bytes 13369344 | tf_op jit(solution)/shard_map/reduce_scatter | solution.py:119
  113.8 3.6 %copy-start.2 = (bf16[1,192,8192]{2,1,0:T(8,128)(2,1)S(1)}, bf16[1,192,8192]{2,1,0:T(8,128)(2,1)}, u32[]{:S(2)}) copy-start(bf16[1,192,8192]{2,1,0:T(8,128)(2,1)} %param.10) | copy-start | bytes 9437188
  237.3 3.3 copy-start.1
  249.2 22.3 %copy-start.5 = (f32[512,128]{1,0:T(8,128)S(1)}, f32[512,128]{1,0:T(8,128)}, u32[]{:S(2)}) copy-start(f32[512,128]{1,0:T(8,128)} %param.16) | copy-start | bytes 786436
Sparse Core Ops, SparseCore 0:
  10.7 81.8 all-gather.4
  108.6 63.1 reduce-scatter.3
  175.0 62.2 reduce-scatter.5
  249.4 83.4 reduce-scatter.7
Sparse Core Ops, SparseCore 1:
  116.4 155.0 all-reduce.1
where the time goes:
time: 345 us; the launch traced here: 342 us
  waiting for transfers between devices  206 us (60%)
  blocking collectives  51.8 us (15%)
  matrix products  51.3 us (15%)
  between operations  15.4 us (4%)
  other arithmetic  14.4 us (4%)
    reduce_scatter x1, waiting for transfers between devices, body(): lax.psum_scatter(value_term.astype(jnp.bfloat16), 'fsdp', scatter_dimensi...  64.2 us
    reduce_scatter x1, waiting for transfers between devices, body(): lax.psum_scatter(jnp.concatenate([qkv_term, out_term], axis=1).astype(jnp...  51.3 us
    reduce_scatter x1, waiting for transfers between devices, body(): lax.psum_scatter(key_term.astype(jnp.bfloat16), 'fsdp', scatter_dimension...  42.8 us
    all_gather x1, blocking collectives, body(): lax.all_gather(key_states[0], 'fsdp', axis=0, tiled=True)  27.2 us
    all_gather x1, blocking collectives, body(): lax.all_gather(value_states[0], 'fsdp', axis=0, tiled=True)  24.6 us
    all_gather x1, waiting for transfers between devices, body(): full_weights = lax.all_gather(weights[0], 'fsdp', axis=0, tiled=True)  24.4 us
    psum x1, waiting for transfers between devices, body(): lax.psum(frag_delta[0].astype(jnp.bfloat16), 'replica').astype(jnp.float32)  22.3 us
    dot_general x1, matrix products, body(): jnp.einsum('htk,thd->kd', score_grad, own_queries, preferred_element_type...  8.69 us
  transfers between devices with their start and end apart: 5, of which 5 were waited for; matrix products, arithmetic and copies ran while one was open for 15% of the time, Pallas kernels for 0%

commit v1 on v0

v1 whole, which is shorter than its diff:
```python
import functools
import math

import jax
import jax.numpy as jnp
from jax import lax
from jax.experimental import pallas as pl
from jax.experimental.pallas import tpu as pltpu
from jax.sharding import PartitionSpec as P

rope_base = 500000.0
outer_rate = 0.7
outer_beta = 0.9
masked_score = -1e30

BF = jnp.bfloat16
F32 = jnp.float32
MESH = pl.DeviceIdType.MESH

TOK = 192
PAIR = 2 * TOK
HD = 128
QW = 256
BLK = 512
WC = 768
QKV = 512
CHIPS = 8
YS = 4

GA = 288
SA = 144
SA1 = 64
SB1 = 208
PART = 256

NT = (((1,), (1,)), ((), ()))
TN = (((0,), (0,)), ((), ()))


def dot(a, b):
    return jnp.dot(a, b, preferred_element_type=F32)


def dot_nt(a, b):
    return lax.dot_general(a, b, NT, preferred_element_type=F32)


def dot_tn(a, b):
    return lax.dot_general(a, b, TN, preferred_element_type=F32)


def kernel(
    replicas,
    inputs,
    out_grad,
    queries,
    keys,
    values,
    weights,
    delta,
    params,
    moment,
    cosines,
    sines,
    input_out,
    weight_out,
    params_out,
    moment_out,
    xi,
    xg,
    wg,
    kb,
    vb,
    qs,
    st,
    plow,
    row_sum,
    att_t,
    dq_t,
    gs,
    agp,
    agr,
    att,
    proj,
    dkv,
    sk,
    ps,
    rk,
    dw,
    rz,
    ra1,
    ra2,
    rb1,
    rb2,
    rf,
    rg,
    rw,
    ig,
    wout,
    cs,
    sn,
    fd,
    fb,
    fr,
    fz,
    fzr,
    fs,
    fp,
    fm,
    lsem,
    ssem,
    rsem,
    bsem,
    brsem,
):
    r = lax.axis_index("replica")
    f = lax.axis_index("fsdp")
    c = lax.rem(f, 2)
    y = lax.rem(f // 2, YS)
    z = f // (2 * YS)
    o = 1 - c
    x = lax.rem(r, 4)
    zh = r // 4

    def chip(dz, dy):
        return lax.rem(z + dz, 2) * YS + lax.rem(y + dy, YS)

    def at(dz, dy, core=None):
        return (r, chip(dz, dy) * 2 + (c if core is None else core))

    yp, ym, zp, sib = at(0, 1), at(0, 3), at(1, 0), at(0, 0, o)

    def back(s):
        return (s // 4) * 4 + (4 - s % 4) % 4

    made = []

    def remote(src, dst, dev):
        i = len(made)
        copy = pltpu.make_async_remote_copy(
            src_ref=src,
            dst_ref=dst,
            send_sem=ssem.at[i],
            recv_sem=rsem.at[i],
            device_id=dev,
            device_id_type=MESH,
        )
        made.append(copy)
        return copy

    local_made = []

    def local(src, dst):
        copy = pltpu.make_async_copy(src, dst, lsem.at[len(local_made)])
        local_made.append(copy)
        copy.start()
        return copy

    def slot_chip(s):
        return lax.rem(z + s // 4, 2) * YS + lax.rem(y + s % 4, YS)

    def columns(s, core):
        return pl.ds(pl.multiple_of((slot_chip(s) * 2 + core) * BLK, BLK), BLK)

    load_q = [local(queries.at[0, :, pl.ds(h * HD, HD)], qs.at[pl.ds(h * TOK, TOK)]) for h in (0, 1)]
    load_k = local(keys.at[0], kb.at[0, c])
    load_v = local(values.at[0], vb.at[0, c])
    load_w = local(weights.at[0], wg.at[0])
    load_d = local(delta.at[0], fd)
    load_g = [local(out_grad.at[0, :, columns(s, c)], xg.at[s, c]) for s in range(CHIPS)]
    load_x = [local(inputs.at[0, :, columns(s, c)], xi.at[s, c]) for s in range(CHIPS)]
    load_t = [local(cosines, cs), local(sines, sn), local(params, fp), local(moment, fm)]

    peers = [at(s // 4, s % 4) for s in range(1, CHIPS)] + [sib]
    x_peers = [(zh * 4 + lax.rem(x + d, 4), f) for d in (1, 2, 3)]
    z_peers = [(lax.rem(zh + d, 4) * 4 + x, f) for d in (1, 2, 3)]
    barrier = pltpu.get_barrier_semaphore()
    for dev in peers + x_peers + z_peers:
        pl.semaphore_signal(barrier, inc=1, device_id=dev, device_id_type=MESH)
    pl.semaphore_wait(barrier, len(peers) + 6)

    order = (1, 3, 4, 5, 7, 2, 6)
    send_k = {back(s): remote(keys.at[0], kb.at[back(s), c], at(s // 4, s % 4)) for s in order}
    send_v = {back(s): remote(values.at[0], vb.at[back(s), c], at(s // 4, s % 4)) for s in order}
    for copy in send_k.values():
        copy.start()
    for copy in send_v.values():
        copy.start()
    cross_k = [remote(keys.at[0], kb.at[0, c], sib)]
    cross_v = [remote(values.at[0], vb.at[0, c], sib)]
    cross_k[0].start()
    cross_v[0].start()

    class Gather:
        def __init__(self, first, width):
            cols = pl.ds(first, width)
            own = weights.at[0, :, cols]

            def rows(s, lo, hi):
                return wg.at[s, pl.ds(lo, hi - lo), cols]

            def move(src, dst, lo, hi, dev):
                return remote(rows(src, lo, hi), rows(dst, lo, hi), dev)

            self.s3 = remote(own, wg.at[3, :, cols], yp)
            self.s1 = remote(own, wg.at[1, :, cols], ym)
            self.s4 = remote(own, wg.at[4, :, cols], zp)
            half = GA // 2
            self.s2a = move(1, 2, 0, BLK // 2, ym)
            self.s2b = move(3, 2, BLK // 2, BLK, yp)
            self.s5b = move(1, 5, GA, BLK, zp)
            self.s7b = move(3, 7, GA, BLK, zp)
            self.s7a = move(4, 7, 0, GA, yp)
            self.s5a = move(4, 5, 0, GA, ym)
            self.s6b = move(2, 6, GA, BLK, zp)
            self.s6a1 = move(5, 6, 0, half, ym)
            self.s6a2 = move(7, 6, half, GA, yp)

        def wave0(self):
            self.s3.start()
            self.s1.start()
            self.s4.start()

        def wave1(self):
            self.s1.wait_recv()
            self.s2a.start()
            self.s5b.start()
            self.s3.wait_recv()
            self.s2b.start()
            self.s7b.start()
            self.s4.wait_recv()
            self.s7a.start()
            self.s5a.start()

        def wave2(self):
            self.s2a.wait_recv()
            self.s2b.wait_recv()
            self.s6b.start()
            self.s5a.wait_recv()
            self.s6a1.start()
            self.s7a.wait_recv()
            self.s6a2.start()

        def finish(self):
            for copy in (self.s5b, self.s7b, self.s6b, self.s6a1, self.s6a2):
                copy.wait_recv()

    gather_o = Gather(QKV, QW)
    gather_q = Gather(0, QW)
    gather_k = Gather(QW, QW)
    gather_o.wave0()

    cross_g = [remote(out_grad.at[0, :, columns(s, o)], xg.at[s, c], sib) for s in range(CHIPS)]
    cross_x = [remote(inputs.at[0, :, columns(s, o)], xi.at[s, c], sib) for s in range(CHIPS)]
    for copy in cross_g:
        copy.start()

    load_d.wait()
    for j in range(4):
        fb[j] = fd[pl.ds(j * 128, 128), :].astype(BF)
    frag_x = [remote(fb.at[lax.rem(x + d, 4)], fr.at[d - 1], x_peers[d - 1]) for d in (1, 2, 3)]
    for copy in frag_x:
        copy.start()

    for copy in load_q:
        copy.wait()
    load_k.wait()
    load_v.wait()
    load_w.wait()
    for s in order:
        send_k[s].wait_recv()
        cross_k.append(remote(kb.at[s, c], kb.at[s, c], sib))
        cross_k[-1].start()
    for copy in cross_k:
        copy.wait_recv()

    scale = 1.0 / math.sqrt(HD)

    def score_step(s, peak):
        part = dot_nt(kb[s].reshape(PAIR, HD), qs[...]) * scale
        key_pos = slot_chip(s) * PAIR + lax.broadcasted_iota(jnp.int32, (PAIR, PAIR), 0)
        lane = lax.broadcasted_iota(jnp.int32, (1, PAIR), 1)
        query_pos = f * TOK + jnp.where(lane >= TOK, lane - TOK, lane)
        part = jnp.where(key_pos <= query_pos, part, masked_score)
        st[s] = part
        return jnp.maximum(peak, jnp.max(part, axis=0, keepdims=True))

    peak = lax.fori_loop(0, CHIPS, score_step, jnp.full((1, PAIR), masked_score, F32))

    def exp_step(s, total):
        part = jnp.exp(st[s] - peak)
        st[s] = part
        return total + jnp.sum(part, axis=0, keepdims=True)

    total = lax.fori_loop(0, CHIPS, exp_step, jnp.zeros((1, PAIR), F32))
    inverse = 1.0 / total

    for s in order:
        send_v[s].wait_recv()
        cross_v.append(remote(vb.at[s, c], vb.at[s, c], sib))
        cross_v[-1].start()
    for copy in cross_v:
        copy.wait_recv()

    att_t[...] = jnp.zeros_like(att_t)

    def value_step(s, carry):
        part = st[s] * inverse
        st[s] = part
        low = part.astype(BF)
        plow[s] = low
        att_t[...] += dot_tn(vb[s].reshape(PAIR, HD), low)
        return carry

    lax.fori_loop(0, CHIPS, value_step, 0)

    attended = att_t[...].T.astype(BF)
    for h in (0, 1):
        att[c, :, pl.ds(h * HD, HD)] = attended[h * TOK : (h + 1) * TOK]
    cross_a = remote(att.at[c], att.at[c], sib)
    cross_a.start()

    for copy in frag_x:
        copy.wait_recv()
    partial = fd[pl.ds(pl.multiple_of(x * 128, 128), 128), :]
    for d in range(3):
        partial = partial + fr[d].astype(F32)
    fs[...] = partial
    fz[...] = partial.astype(BF).reshape(4, 32, 128)
    frag_z = [remote(fz.at[lax.rem(zh + d, 4)], fzr.at[d - 1], z_peers[d - 1]) for d in (1, 2, 3)]
    for copy in frag_z:
        copy.start()

    gather_o.wave1()
    gather_o.wave2()
    gather_q.wave0()
    for copy in cross_x:
        copy.start()

    for copy in load_g:
        copy.wait()
    for copy in cross_g:
        copy.wait_recv()
    gather_o.finish()
    agp[...] = jnp.zeros_like(agp)

    def grad_step(s, carry):
        part = dot(xg[s].reshape(PAIR, BLK), wg[s, :, pl.ds(QKV, QW)])
        agp[...] += part.reshape(2, TOK, QW)
        return carry

    lax.fori_loop(0, CHIPS, grad_step, 0)
    cross_p = remote(agp.at[o], agr, sib)
    cross_p.start()
    cross_p.wait_recv()
    grad = (agp[c] + agr[...]).astype(BF)
    for h in (0, 1):
        gs[pl.ds(h * TOK, TOK), :] = grad[:, h * HD : (h + 1) * HD]
    row_delta = jnp.sum(att_t[...] * gs[...].astype(F32).T, axis=0, keepdims=True)

    gather_q.wave1()

    dq_t[...] = jnp.zeros_like(dq_t)

    def cross_copy(s):
        return pltpu.make_async_remote_copy(
            src_ref=dkv.at[s, o],
            dst_ref=sk.at[s],
            send_sem=bsem.at[s],
            recv_sem=brsem.at[s],
            device_id=sib,
            device_id_type=MESH,
        )

    def back_step(s, carry):
        prob_grad = dot_nt(vb[s].reshape(PAIR, HD), gs[...])
        low = (st[s] * (prob_grad - row_delta) * scale).astype(BF)
        dq_t[...] += dot_tn(kb[s].reshape(PAIR, HD), low)
        dkv[s, :, :, pl.ds(0, HD)] = dot(low, qs[...]).astype(BF).reshape(2, TOK, HD)
        dkv[s, :, :, pl.ds(HD, HD)] = dot(plow[s], gs[...]).astype(BF).reshape(2, TOK, HD)
        cross_copy(s).start()
        return carry

    lax.fori_loop(0, CHIPS, back_step, 0)

    def pair_step(s, carry):
        cross_copy(s).wait_recv()
        ps[s] = (dkv[s, c].astype(F32) + sk[s].astype(F32)).astype(BF)
        return carry

    lax.fori_loop(0, CHIPS, pair_step, 0)
    send_d = {back(s): remote(ps.at[s], rk.at[back(s)], at(s // 4, s % 4)) for s in order}
    for copy in send_d.values():
        copy.start()
    gather_q.wave2()
    gather_k.wave0()

    for copy in load_t:
        copy.wait()

    def rotate(values_in):
        return values_in * cs[...] + pltpu.roll(values_in, HD // 2, 1) * sn[...]

    dq = dq_t[...].T
    for h in (0, 1):
        proj[c, :, pl.ds(h * HD, HD)] = rotate(dq[h * TOK : (h + 1) * TOK]).astype(BF)
    cross_q = remote(proj.at[c, :, pl.ds(0, QW)], proj.at[c, :, pl.ds(0, QW)], sib)
    cross_q.start()

    class Scatter:
        def __init__(self, p):
            self.p = p
            part = dw.at[p]
            self.to_z = remote(part.at[pl.ds(4, 4), pl.ds(SA, PART - SA)], rz.at[p], zp)
            self.a_up = [remote(part.at[s, pl.ds(0, SA1)], ra1.at[p, i], yp) for i, s in enumerate((2, 6))]
            self.a_down = [
                remote(part.at[s, pl.ds(SA1, SA - SA1)], ra2.at[p, i], ym) for i, s in enumerate((2, 6))
            ]
            self.b_up = remote(part.at[2, pl.ds(SA, SB1 - SA)], rb1.at[p], yp)
            self.b_down = remote(part.at[2, pl.ds(SB1, PART - SB1)], rb2.at[p], ym)
            self.f_up = remote(part.at[1], rf.at[p, 0], yp)
            self.g_up = remote(part.at[5, pl.ds(0, SA)], rg.at[p, 0], yp)
            self.f_down = remote(part.at[3], rf.at[p, 1], ym)
            self.g_down = remote(part.at[7, pl.ds(0, SA)], rg.at[p, 1], ym)
            self.last = remote(part.at[4, pl.ds(0, SA)], rw.at[p], zp)

        def add(self, s, lo, hi, *others):
            rows = pl.ds(lo, hi - lo)
            value = dw[self.p, s, rows, :].astype(F32)
            for other in others:
                value = value + other[...].astype(F32)
            dw[self.p, s, rows, :] = value.astype(BF)

        def step1(self):
            self.to_z.start()
            for copy in self.a_up + self.a_down:
                copy.start()

        def step2(self):
            self.to_z.wait_recv()
            self.add(2, SA, PART, rz.at[self.p, 2])
            self.b_up.start()
            self.b_down.start()
            for s in (1, 3, 0):
                self.add(s, SA, PART, rz.at[self.p, s])

        def step3(self):
            p = self.p
            for copy in self.a_up + [self.b_up]:
                copy.wait_recv()
            self.add(5, 0, SA1, ra1.at[p, 1])
            self.g_up.start()
            self.add(1, 0, SA1, ra1.at[p, 0])
            self.add(1, SA, SB1, rb1.at[p])
            self.f_up.start()
            for copy in self.a_down + [self.b_down]:
                copy.wait_recv()
            self.add(7, SA1, SA, ra2.at[p, 1])
            self.g_down.start()
            self.add(3, SA1, SA, ra2.at[p, 0])
            self.add(3, SB1, PART, rb2.at[p])
            self.f_down.start()

        def step4(self):
            self.g_up.wait_recv()
            self.g_down.wait_recv()
            self.add(4, 0, SA, rg.at[self.p, 0], rg.at[self.p, 1])
            self.last.start()

        def step5(self, first):
            p = self.p
            self.f_up.wait_recv()
            self.f_down.wait_recv()
            self.last.wait_recv()
            value = dw[p, 0].astype(F32) + rf[p, 0].astype(F32) + rf[p, 1].astype(F32)
            top = value[:SA] + rw[p].astype(F32)
            value = jnp.concatenate([top, value[SA:]], axis=0)
            wout[:, pl.ds(first, PART)] = value.T.astype(BF)

    scatter_o, scatter_q, scatter_k = Scatter(0), Scatter(1), Scatter(2)

    def outer(p, left, right):
        def step(s, carry):
            dw[p, s] = dot(left, right[s].reshape(PAIR, BLK)).astype(BF)
            return carry

        lax.fori_loop(0, CHIPS, step, 0)

    cross_a.wait_recv()
    outer(0, att[...].reshape(PAIR, QW).T, xg)

    for copy in frag_z:
        copy.wait_recv()
    own = fs[pl.ds(pl.multiple_of(zh * 32, 32), 32), :]
    for d in range(3):
        own = own + fzr[d].astype(F32)
    fs[pl.ds(pl.multiple_of(zh * 32, 32), 32), :] = own
    home_z = pl.ds(pl.multiple_of(zh * 32, 32), 32)
    frag_bz = [remote(fs.at[home_z], fs.at[home_z], dev) for dev in z_peers]
    for copy in frag_z:
        copy.wait_send()
    for copy in frag_bz:
        copy.start()

    gather_k.wave1()
    scatter_o.step1()

    for copy in load_x:
        copy.wait()
    for copy in cross_x:
        copy.wait_recv()
    cross_q.wait_recv()
    outer(1, proj[:, :, pl.ds(0, QW)].reshape(PAIR, QW).T, xi)
    gather_k.wave2()
    scatter_q.step1()

    for copy in send_d.values():
        copy.wait_recv()

    def sum_step(s, carry):
        return carry + rk[s].astype(F32)

    kv = lax.fori_loop(1, CHIPS, sum_step, ps[0].astype(F32))
    proj[c, :, pl.ds(QW, HD)] = rotate(kv[:, :HD]).astype(BF)
    proj[c, :, pl.ds(QW + HD, HD)] = kv[:, HD:].astype(BF)
    cross_kv = remote(proj.at[c, :, pl.ds(QW, QW)], proj.at[c, :, pl.ds(QW, QW)], sib)
    cross_kv.start()
    cross_kv.wait_recv()
    outer(2, proj[:, :, pl.ds(QW, QW)].reshape(PAIR, QW).T, xi)
    scatter_k.step1()

    for copy in frag_bz:
        copy.wait_recv()
    home_x = pl.ds(pl.multiple_of(x * 128, 128), 128)
    for copy in frag_bz:
        copy.wait_send()
    fd[home_x, :] = fs[...]
    frag_bx = [remote(fs, fd.at[home_x], dev) for dev in x_peers]
    for copy in frag_bx:
        copy.start()

    scatter_o.step2()
    gather_q.finish()
    gather_k.finish()

    for s in range(CHIPS):
        ig[s] = dot_nt(proj[...].reshape(PAIR, QKV), wg[s, :, pl.ds(0, QKV)]).astype(BF).reshape(2, TOK, BLK)
        local(ig.at[s, c], input_out.at[0, :, columns(s, c)])
    grad_stores = local_made[-CHIPS:]
    cross_i = [
        remote(ig.at[s, o], input_out.at[0, :, columns(s, c)], sib) for s in range(CHIPS)
    ]
    for copy in cross_i:
        copy.start()

    scatter_o.step3()
    scatter_q.step2()
    scatter_o.step4()
    scatter_q.step3()
    scatter_k.step2()
    scatter_o.step5(QKV)
    scatter_q.step4()
    scatter_k.step3()
    scatter_q.step5(0)
    scatter_k.step4()

    for copy in frag_bx:
        copy.wait_recv()
    outer_grad = fd[...] / replicas
    moment_next = outer_beta * fm[...] + outer_grad
    fm[...] = moment_next
    fp[...] = fp[...] - outer_rate * (outer_grad + outer_beta * moment_next)
    stores = [local(fm, moment_out), local(fp, params_out)]

    scatter_k.step5(QW)
    stores.append(local(wout, weight_out.at[0]))

    for copy in cross_i:
        copy.wait_recv()
    for copy in grad_stores + stores:
        copy.wait()
    waited = frag_z + frag_bz
    for copy in made:
        if not any(copy is other for other in waited):
            copy.wait_send()

    def drain(s, carry):
        cross_copy(s).wait_send()
        return carry

    lax.fori_loop(0, CHIPS, drain, 0)


def body(inputs, out_grad, queries, key_states, value_states, weights, frag_delta, frag_params, frag_moment):
    half = HD // 2
    inverse_freq = jnp.exp(-math.log(rope_base) * 2.0 * jnp.arange(half, dtype=F32) / HD)
    positions = lax.axis_index("fsdp") * TOK + jnp.arange(TOK, dtype=jnp.int32)
    angles = positions.astype(F32)[:, None] * inverse_freq[None, :]
    cosine, sine = jnp.cos(angles), jnp.sin(angles)
    cosines = jnp.concatenate([cosine, cosine], axis=1)
    sines = jnp.concatenate([sine, -sine], axis=1)
    anywhere = pl.BlockSpec(memory_space=pl.ANY)
    vm = pltpu.VMEM
    dma = pltpu.SemaphoreType.DMA
    return pl.pallas_call(
        functools.partial(kernel, float(lax.axis_size("replica"))),
        out_shape=(
            jax.ShapeDtypeStruct(inputs.shape, BF),
            jax.ShapeDtypeStruct(weights.shape, BF),
            jax.ShapeDtypeStruct(frag_params.shape, F32),
            jax.ShapeDtypeStruct(frag_moment.shape, F32),
        ),
        in_specs=[anywhere] * 11,
        out_specs=(anywhere,) * 4,
        scratch_shapes=[
            vm((CHIPS, 2, TOK, BLK), BF),
            vm((CHIPS, 2, TOK, BLK), BF),
            vm((CHIPS, BLK, WC), BF),
            vm((CHIPS, 2, TOK, HD), BF),
            vm((CHIPS, 2, TOK, HD), BF),
            vm((PAIR, HD), BF),
            vm((CHIPS, PAIR, PAIR), F32),
            vm((CHIPS, PAIR, PAIR), BF),
            vm((1, PAIR), F32),
            vm((HD, PAIR), F32),
            vm((HD, PAIR), F32),
            vm((PAIR, HD), BF),
            vm((2, TOK, QW), F32),
            vm((TOK, QW), F32),
            vm((2, TOK, QW), BF),
            vm((2, TOK, QKV), BF),
            vm((CHIPS, 2, TOK, QW), BF),
            vm((CHIPS, TOK, QW), BF),
            vm((CHIPS, TOK, QW), BF),
            vm((CHIPS, TOK, QW), BF),
            vm((3, CHIPS, PART, BLK), BF),
            vm((3, YS, PART - SA, BLK), BF),
            vm((3, 2, SA1, BLK), BF),
            vm((3, 2, SA - SA1, BLK), BF),
            vm((3, SB1 - SA, BLK), BF),
            vm((3, PART - SB1, BLK), BF),
            vm((3, 2, PART, BLK), BF),
            vm((3, 2, SA, BLK), BF),
            vm((3, SA, BLK), BF),
            vm((CHIPS, 2, TOK, BLK), BF),
            vm((BLK, WC), BF),
            vm((TOK, HD), F32),
            vm((TOK, HD), F32),
            vm((512, 128), F32),
            vm((4, 128, 128), BF),
            vm((3, 128, 128), BF),
            vm((4, 32, 128), BF),
            vm((3, 32, 128), BF),
            vm((128, 128), F32),
            vm((512, 128), F32),
            vm((512, 128), F32),
            dma((64,)),
            dma((192,)),
            dma((192,)),
            dma((CHIPS,)),
            dma((CHIPS,)),
        ],
        compiler_params=pltpu.CompilerParams(
            collective_id=0, has_side_effects=True, vmem_limit_bytes=60 * 2**20
        ),
    )(inputs, out_grad, queries, key_states, value_states, weights, frag_delta, frag_params, frag_moment, cosines, sines)


def solution(mesh):
    rows = P("replica", "fsdp", None)
    shared = P("fsdp", None)
    return jax.shard_map(
        body,
        mesh=mesh,
        in_specs=(rows,) * 7 + (shared,) * 2,
        out_specs=(rows, rows, shared, shared),
        check_vma=False,
    )
```

time: 345 us -> 135 us (0.39)
  waiting for transfers between devices: 206 us -> 0 us
  Pallas kernels: 0 us -> 125 us
  blocking collectives: 51.8 us -> 0 us
  matrix products: 51.3 us -> 0 us
  between operations: 15.4 us -> 0.69 us
  other arithmetic: 14.4 us -> 1.24 us
    reduce_scatter x3 -> x0, waiting for transfers between devices: 158 us -> none  [the longest x1 64.2 us: body(): lax.psum_scatter(value_term.astype(jnp.bfloat16), 'fsdp', scatter_dimensi...]
    pallas_call x0 -> x1, Pallas kernels: none -> 125 us  [body(): pl.pallas_call(functools.partial(kernel, float(lax.axis_size('replica')))...]
    all_gather x2 -> x0, blocking collectives: 51.8 us -> none  [the longest x1 27.2 us: body(): lax.all_gather(key_states[0], 'fsdp', axis=0, tiled=True)]
    dot_general x9 -> x0, matrix products: 46 us -> none  [the longest x1 8.69 us: body(): jnp.einsum('htk,thd->kd', score_grad, own_queries, preferred_element_type...]
    all_gather x1 -> x0, waiting for transfers between devices: 24.4 us -> none  [body(): full_weights = lax.all_gather(weights[0], 'fsdp', axis=0, tiled=True)]
    psum x1 -> x0, waiting for transfers between devices: 22.3 us -> none  [body(): lax.psum(frag_delta[0].astype(jnp.bfloat16), 'replica').astype(jnp.float32)]
    concatenate x1, other arithmetic: 8.59 us -> 0.8 us  [body(): cosines = jnp.concatenate([cosine, cosine], axis=1)]
    sub x1 -> x0, matrix products: 5.3 us -> none  [body(): exponent = jnp.exp(scores - row_peak)]
  transfers between devices with their start and end apart: 5 -> 0, of which waited for: 5 -> 0; matrix products, arithmetic and copies ran while one was open for 15% -> 0% of each run, Pallas kernels for 0% -> 0%
where the time goes in v1:
time: 135 us; the launch traced here: 133 us
  Pallas kernels  125 us (93%)
  local copies, waits for them, and re-layouts  6.25 us (5%)
    pallas_call x1, Pallas kernels, body(): pl.pallas_call(functools.partial(kernel, float(lax.axis_size('replica')))...  125 us
    unnamed x10, local copies, waits for them, and re-layouts  6.25 us

profile of v1, /device:TPU:1, one launch (start us, length us, event | category | flops | bytes accessed | tf_op | source)
XLA Modules:
  0.0 133.1 jit_solution(3446488520693679070)
XLA Ops:
  0.7 0.4 multiply_sine_fusion
  1.1 0.8 pad_maximum_fusion
  1.9 124.9 %shard_map.120 = (bf16[1,192,8192]{2,1,0:T(8,128)(2,1)}, bf16[1,512,768]{2,1,0:T(8,128)(2,1)}, f32[512,128]{1,0:T(8,128)}, f32[512,128]{1,0:T(8,128)}) custom-call(bf16[1,192,8192]{2,1,0:T(8,128)(2,1)} %inputs.1, bf16[1,192,8192]{2,1,0:T(8,128)(2,1)} %out_grad.1, bf16[1,192,256]{2,1,0:T(8,128)(2,1)} %queries.1, bf16[1,192,128]{2,1,0:T(8,128)(2,1)} %keys.1, ...), custom_call_target="tpu_custom_call" | custom-call | tf_op jit(solution)/shard_map/pallas_call | solution.py:605
  126.8 0.0 copy-start
  126.8 0.0 copy-start.2
  126.8 0.0 copy-start.1
  126.8 4.0 %copy.17 = bf16[1,192,8192]{2,1,0:T(8,128)(2,1)} copy(bf16[1,192,8192]{2,1,0:T(8,128)(2,1)} %get-tuple-element.13) | data formatting | bytes 6291456
  130.8 0.0 copy-done
  130.8 0.9 copy.18
  131.7 0.0 copy-done.2
  131.7 0.7 copy.19
  132.4 0.0 copy-done.1
  132.4 0.7 copy.20
  (2 shorter events, 0.0 us)
Async XLA Ops:
  126.8 4.0 %copy-start = (bf16[1,512,768]{2,1,0:T(8,128)(2,1)S(1)}, bf16[1,512,768]{2,1,0:T(8,128)(2,1)}, u32[]{:S(2)}) copy-start(bf16[1,512,768]{2,1,0:T(8,128)(2,1)} %get-tuple-element.14) | copy-start | bytes 2359300
  126.8 4.9 %copy-start.2 = (f32[512,128]{1,0:T(8,128)S(1)}, f32[512,128]{1,0:T(8,128)}, u32[]{:S(2)}) copy-start(f32[512,128]{1,0:T(8,128)} %get-tuple-element.15) | copy-start | bytes 786436
  126.8 5.6 %copy-start.1 = (f32[512,128]{1,0:T(8,128)S(1)}, f32[512,128]{1,0:T(8,128)}, u32[]{:S(2)}) copy-start(f32[512,128]{1,0:T(8,128)} %get-tuple-element.16) | copy-start | bytes 786436

commit v2 on v1

v2 whole, which is shorter than its diff:
```python
import functools
import math

import jax
import jax.numpy as jnp
from jax import lax
from jax.experimental import pallas as pl
from jax.experimental.pallas import tpu as pltpu
from jax.sharding import PartitionSpec as P

rope_base = 500000.0
outer_rate = 0.7
outer_beta = 0.9
masked_score = -1e30

BF = jnp.bfloat16
F32 = jnp.float32
MESH = pl.DeviceIdType.MESH

TOK = 192
PAIR = 2 * TOK
HD = 128
QW = 256
BLK = 512
WC = 768
QKV = 512
CHIPS = 8
YS = 4

WEIGHT_Z = 288
KEY_Z = 112
GRAD_Z = (160, 128, 128)
MOST_A, MOST_B = 160, 128
PART = 256

NT = (((1,), (1,)), ((), ()))
TN = (((0,), (0,)), ((), ()))


def dot(a, b):
    return jnp.dot(a, b, preferred_element_type=F32)


def dot_nt(a, b):
    return lax.dot_general(a, b, NT, preferred_element_type=F32)


def dot_tn(a, b):
    return lax.dot_general(a, b, TN, preferred_element_type=F32)


def kernel(
    replicas,
    inputs,
    out_grad,
    queries,
    keys,
    values,
    weights,
    delta,
    params,
    moment,
    input_out,
    weight_out,
    params_out,
    moment_out,
    xi,
    xg,
    wg,
    kb,
    vb,
    qs,
    st,
    plow,
    att_t,
    dq_t,
    gs,
    agp,
    agr,
    att,
    proj,
    dkv,
    sk,
    ps,
    rk,
    dw,
    rz,
    ra1,
    ra2,
    rb1,
    rb2,
    rf,
    rg,
    rw,
    ig,
    cs,
    sn,
    fd,
    fb,
    fr,
    fz,
    fzr,
    fs,
    fp,
    fm,
    lsem,
    ssem,
    rsem,
    bsem,
    brsem,
):
    r = lax.axis_index("replica")
    f = lax.axis_index("fsdp")
    c = lax.rem(f, 2)
    y = lax.rem(f // 2, YS)
    z = f // (2 * YS)
    o = 1 - c
    x = lax.rem(r, 4)
    zh = r // 4

    def chip(dz, dy):
        return lax.rem(z + dz, 2) * YS + lax.rem(y + dy, YS)

    def at(dz, dy, core=None):
        return (r, chip(dz, dy) * 2 + (c if core is None else core))

    yp, ym, zp, sib = at(0, 1), at(0, 3), at(1, 0), at(0, 0, o)

    def back(s):
        return (s // 4) * 4 + (4 - s % 4) % 4

    made = []

    def remote(src, dst, dev):
        i = len(made)
        copy = pltpu.make_async_remote_copy(
            src_ref=src,
            dst_ref=dst,
            send_sem=ssem.at[i],
            recv_sem=rsem.at[i],
            device_id=dev,
            device_id_type=MESH,
        )
        made.append(copy)
        return copy

    local_made = []

    def local(src, dst):
        copy = pltpu.make_async_copy(src, dst, lsem.at[len(local_made)])
        local_made.append(copy)
        copy.start()
        return copy

    def slot_chip(s):
        return lax.rem(z + s // 4, 2) * YS + lax.rem(y + s % 4, YS)

    def columns(s, core):
        return pl.ds(pl.multiple_of((slot_chip(s) * 2 + core) * BLK, BLK), BLK)

    load_q = [local(queries.at[0, :, pl.ds(h * HD, HD)], qs.at[pl.ds(h * TOK, TOK)]) for h in (0, 1)]
    load_k = local(keys.at[0], kb.at[0, c])
    load_v = local(values.at[0], vb.at[0, c])
    load_w = local(weights.at[0], wg.at[0])
    load_d = local(delta.at[0], fd)
    load_g = [local(out_grad.at[0, :, columns(s, c)], xg.at[s, c]) for s in range(CHIPS)]
    load_x = [local(inputs.at[0, :, columns(s, c)], xi.at[s, c]) for s in range(CHIPS)]
    load_t = [local(params, fp), local(moment, fm)]

    peers = [at(s // 4, s % 4) for s in range(1, CHIPS)] + [sib]
    x_peers = [(zh * 4 + lax.rem(x + d, 4), f) for d in (1, 2, 3)]
    z_peers = [(lax.rem(zh + d, 4) * 4 + x, f) for d in (1, 2, 3)]
    barrier = pltpu.get_barrier_semaphore()
    for dev in peers + x_peers + z_peers:
        pl.semaphore_signal(barrier, inc=1, device_id=dev, device_id_type=MESH)
    pl.semaphore_wait(barrier, len(peers) + 6)

    class Gather:
        def __init__(self, own, rows, extent, first):
            def move(src, dst, lo, hi, dev):
                return remote(rows(src, lo, hi), rows(dst, lo, hi), dev)

            half = first // 2
            self.s3 = remote(own, rows(3, 0, extent), yp)
            self.s1 = remote(own, rows(1, 0, extent), ym)
            self.s4 = remote(own, rows(4, 0, extent), zp)
            self.s2a = move(1, 2, 0, extent // 2, ym)
            self.s2b = move(3, 2, extent // 2, extent, yp)
            self.s5b = move(1, 5, first, extent, zp)
            self.s7b = move(3, 7, first, extent, zp)
            self.s7a = move(4, 7, 0, first, yp)
            self.s5a = move(4, 5, 0, first, ym)
            self.s6b = move(2, 6, first, extent, zp)
            self.s6a1 = move(5, 6, 0, half, ym)
            self.s6a2 = move(7, 6, half, first, yp)

        def wave0(self):
            self.s3.start()
            self.s1.start()
            self.s4.start()

        def wave1(self):
            self.s1.wait_recv()
            self.s2a.start()
            self.s5b.start()
            self.s3.wait_recv()
            self.s2b.start()
            self.s7b.start()
            self.s4.wait_recv()
            self.s7a.start()
            self.s5a.start()

        def wave2(self):
            self.s2a.wait_recv()
            self.s2b.wait_recv()
            self.s6b.start()
            self.s5a.wait_recv()
            self.s6a1.start()
            self.s7a.wait_recv()
            self.s6a2.start()

        def finish(self):
            for copy in (self.s5b, self.s7b, self.s6b, self.s6a1, self.s6a2):
                copy.wait_recv()

    def gather_states(source, target):
        return Gather(source.at[0], lambda s, lo, hi: target.at[s, c, pl.ds(lo, hi - lo)], TOK, KEY_Z)

    def gather_weights(first):
        cols = pl.ds(first, HD)
        return Gather(
            weights.at[0, :, cols], lambda s, lo, hi: wg.at[s, pl.ds(lo, hi - lo), cols], BLK, WEIGHT_Z
        )

    order = (1, 3, 4, 5, 7, 2, 6)
    gather_key = gather_states(keys, kb)
    gather_value = gather_states(values, vb)
    gather_o = [gather_weights(QKV + HD * i) for i in range(2)]
    gather_q = [gather_weights(HD * i) for i in range(4)]
    gather_key.wave0()
    gather_value.wave0()
    gather_o[0].wave0()
    gather_o[1].wave0()
    cross_k = [remote(keys.at[0] if s == 0 else kb.at[s, c], kb.at[s, c], sib) for s in range(CHIPS)]
    cross_v = [remote(values.at[0] if s == 0 else vb.at[s, c], vb.at[s, c], sib) for s in range(CHIPS)]

    cross_g = [remote(out_grad.at[0, :, columns(s, o)], xg.at[s, c], sib) for s in range(CHIPS)]
    cross_x = [remote(inputs.at[0, :, columns(s, o)], xi.at[s, c], sib) for s in range(CHIPS)]
    for copy in cross_g:
        copy.start()

    load_d.wait()
    for j in range(4):
        fb[j] = fd[pl.ds(j * 128, 128), :].astype(BF)
    frag_x = [remote(fb.at[lax.rem(x + d, 4)], fr.at[d - 1], x_peers[d - 1]) for d in (1, 2, 3)]
    for copy in frag_x:
        copy.start()

    pos = (f * TOK + lax.broadcasted_iota(jnp.int32, (TOK, HD), 0)).astype(F32)
    lane = lax.broadcasted_iota(jnp.int32, (1, HD), 1)
    step_of = jnp.where(lane >= HD // 2, lane - HD // 2, lane).astype(F32)
    angles = pos * jnp.exp(-math.log(rope_base) * 2.0 * step_of / HD)
    cs[...] = jnp.cos(angles)
    sine = jnp.sin(angles)
    sn[...] = jnp.where(lane >= HD // 2, -sine, sine)

    for copy in load_q:
        copy.wait()
    load_k.wait()
    load_v.wait()
    load_w.wait()
    gather_key.wave1()
    gather_value.wave1()
    gather_o[0].wave1()
    gather_o[1].wave1()
    gather_key.wave2()
    gather_value.wave2()
    gather_q[0].wave0()
    gather_o[0].wave2()
    gather_q[1].wave0()
    gather_o[1].wave2()
    gather_key.finish()
    for copy in cross_k:
        copy.start()
    gather_value.finish()
    for copy in cross_v:
        copy.start()
    for copy in cross_x:
        copy.start()
    for copy in cross_k:
        copy.wait_recv()

    scale = 1.0 / math.sqrt(HD)

    def score_step(s, peak):
        part = dot_nt(kb[s].reshape(PAIR, HD), qs[...]) * scale
        key_pos = slot_chip(s) * PAIR + lax.broadcasted_iota(jnp.int32, (PAIR, PAIR), 0)
        lane = lax.broadcasted_iota(jnp.int32, (1, PAIR), 1)
        query_pos = f * TOK + jnp.where(lane >= TOK, lane - TOK, lane)
        part = jnp.where(key_pos <= query_pos, part, masked_score)
        st[s] = part
        return jnp.maximum(peak, jnp.max(part, axis=0, keepdims=True))

    peak = lax.fori_loop(0, CHIPS, score_step, jnp.full((1, PAIR), masked_score, F32))

    def exp_step(s, total):
        part = jnp.exp(st[s] - peak)
        st[s] = part
        return total + jnp.sum(part, axis=0, keepdims=True)

    total = lax.fori_loop(0, CHIPS, exp_step, jnp.zeros((1, PAIR), F32))
    inverse = 1.0 / total

    gather_q[2].wave0()
    gather_q[0].wave1()
    for copy in cross_v:
        copy.wait_recv()

    att_t[...] = jnp.zeros_like(att_t)

    def value_step(s, carry):
        part = st[s] * inverse
        st[s] = part
        low = part.astype(BF)
        plow[s] = low
        att_t[...] += dot_tn(vb[s].reshape(PAIR, HD), low)
        return carry

    lax.fori_loop(0, CHIPS, value_step, 0)

    attended = att_t[...].T.astype(BF)
    for h in (0, 1):
        att[c, :, pl.ds(h * HD, HD)] = attended[h * TOK : (h + 1) * TOK]
    cross_a = remote(att.at[c], att.at[c], sib)
    cross_a.start()

    for copy in frag_x:
        copy.wait_recv()
    partial = fd[pl.ds(pl.multiple_of(x * 128, 128), 128), :]
    for d in range(3):
        partial = partial + fr[d].astype(F32)
    fs[...] = partial
    fz[...] = partial.astype(BF).reshape(4, 32, 128)
    frag_z = [remote(fz.at[lax.rem(zh + d, 4)], fzr.at[d - 1], z_peers[d - 1]) for d in (1, 2, 3)]
    for copy in frag_z:
        copy.start()

    gather_q[3].wave0()

    class Scatter:
        def __init__(self, p):
            self.p = p
            part = dw.at[p]
            a = self.a = GRAD_Z[p]
            b = PART - a
            a1, self.b1 = a // 2, a + b // 2
            self.a1 = a1
            far = tuple(enumerate((2, 6)))
            top, rest = pl.ds(0, a), pl.ds(a, b)
            self.to_z = remote(part.at[pl.ds(4, 4), rest], rz.at[p, :, pl.ds(0, b)], zp)
            self.a_up = [remote(part.at[s, pl.ds(0, a1)], ra1.at[p, i, pl.ds(0, a1)], yp) for i, s in far]
            self.a_down = [
                remote(part.at[s, pl.ds(a1, a - a1)], ra2.at[p, i, pl.ds(0, a - a1)], ym) for i, s in far
            ]
            self.b_up = remote(part.at[2, pl.ds(a, b // 2)], rb1.at[p, pl.ds(0, b // 2)], yp)
            self.b_down = remote(part.at[2, pl.ds(self.b1, b // 2)], rb2.at[p, pl.ds(0, b // 2)], ym)
            self.g = [
                remote(part.at[5, top], rg.at[p, 0, top], yp),
                remote(part.at[7, top], rg.at[p, 1, top], ym),
            ]
            self.fa = [
                remote(part.at[1, top], rf.at[p, 0, top], yp),
                remote(part.at[3, top], rf.at[p, 1, top], ym),
            ]
            self.fb = [
                remote(part.at[1, rest], rf.at[p, 0, rest], yp),
                remote(part.at[3, rest], rf.at[p, 1, rest], ym),
            ]
            self.last = remote(part.at[4, top], rw.at[p, top], zp)

        def add(self, s, lo, hi, *others):
            rows = pl.ds(lo, hi - lo)
            value = dw[self.p, s, rows, :].astype(F32)
            for other in others:
                value = value + other[...].astype(F32)
            dw[self.p, s, rows, :] = value.astype(BF)

        def begin(self):
            for copy in self.a_up + self.a_down:
                copy.start()
            self.to_z.start()

        def a_near(self):
            p, a, a1 = self.p, self.a, self.a1
            for copy in self.a_up:
                copy.wait_recv()
            self.add(5, 0, a1, ra1.at[p, 1, pl.ds(0, a1)])
            self.g[0].start()
            self.add(1, 0, a1, ra1.at[p, 0, pl.ds(0, a1)])
            self.fa[0].start()
            for copy in self.a_down:
                copy.wait_recv()
            self.add(7, a1, a, ra2.at[p, 1, pl.ds(0, a - a1)])
            self.g[1].start()
            self.add(3, a1, a, ra2.at[p, 0, pl.ds(0, a - a1)])
            self.fa[1].start()

        def a_last(self):
            p, a = self.p, self.a
            for copy in self.g:
                copy.wait_recv()
            self.add(4, 0, a, rg.at[p, 0, pl.ds(0, a)], rg.at[p, 1, pl.ds(0, a)])
            self.last.start()

        def b_far(self):
            p, a = self.p, self.a
            b = PART - a
            self.to_z.wait_recv()
            self.add(2, a, PART, rz.at[p, 2, pl.ds(0, b)])
            self.b_up.start()
            self.b_down.start()
            for s in (1, 3, 0):
                self.add(s, a, PART, rz.at[p, s, pl.ds(0, b)])

        def b_near(self):
            p, a, b1 = self.p, self.a, self.b1
            half = b1 - a
            self.b_up.wait_recv()
            self.add(1, a, b1, rb1.at[p, pl.ds(0, half)])
            self.fb[0].start()
            self.b_down.wait_recv()
            self.add(3, b1, PART, rb2.at[p, pl.ds(0, half)])
            self.fb[1].start()

        def end(self, first):
            p, a = self.p, self.a
            for copy in self.fa + self.fb + [self.last]:
                copy.wait_recv()
            value = dw[p, 0].astype(F32) + rf[p, 0].astype(F32) + rf[p, 1].astype(F32)
            top = value[:a] + rw[p, pl.ds(0, a), :].astype(F32)
            value = jnp.concatenate([top, value[a:]], axis=0)
            weight_out[0, :, pl.ds(first, PART)] = value.T.astype(BF)

    scatter_o, scatter_q, scatter_k = Scatter(0), Scatter(1), Scatter(2)

    def outer(p, left, right):
        def step(s, carry):
            dw[p, s] = dot(left, right[s].reshape(PAIR, BLK)).astype(BF)
            return carry

        lax.fori_loop(0, CHIPS, step, 0)

    for copy in load_g:
        copy.wait()
    for copy in cross_g:
        copy.wait_recv()
    gather_o[0].finish()
    gather_o[1].finish()
    agp[...] = jnp.zeros_like(agp)

    def grad_step(s, carry):
        part = dot(xg[s].reshape(PAIR, BLK), wg[s, :, pl.ds(QKV, QW)])
        agp[...] += part.reshape(2, TOK, QW)
        return carry

    lax.fori_loop(0, CHIPS, grad_step, 0)
    cross_p = remote(agp.at[o], agr, sib)
    cross_p.start()
    gather_q[2].wave1()
    gather_q[1].wave1()
    gather_q[0].wave2()
    cross_a.wait_recv()
    outer(0, att[...].reshape(PAIR, QW).T, xg)
    scatter_o.begin()
    cross_p.wait_recv()
    grad = (agp[c] + agr[...]).astype(BF)
    for h in (0, 1):
        gs[pl.ds(h * TOK, TOK), :] = grad[:, h * HD : (h + 1) * HD]
    row_delta = jnp.sum(att_t[...] * gs[...].astype(F32).T, axis=0, keepdims=True)

    dq_t[...] = jnp.zeros_like(dq_t)

    def cross_copy(s):
        return pltpu.make_async_remote_copy(
            src_ref=dkv.at[s, o],
            dst_ref=sk.at[s],
            send_sem=bsem.at[s],
            recv_sem=brsem.at[s],
            device_id=sib,
            device_id_type=MESH,
        )

    def back_step(s, carry):
        prob_grad = dot_nt(vb[s].reshape(PAIR, HD), gs[...])
        low = (st[s] * (prob_grad - row_delta) * scale).astype(BF)
        dq_t[...] += dot_tn(kb[s].reshape(PAIR, HD), low)
        dkv[s, :, :, pl.ds(0, HD)] = dot(low, qs[...]).astype(BF).reshape(2, TOK, HD)
        dkv[s, :, :, pl.ds(HD, HD)] = dot(plow[s], gs[...]).astype(BF).reshape(2, TOK, HD)
        cross_copy(s).start()
        return carry

    lax.fori_loop(0, CHIPS, back_step, 0)

    gather_q[3].wave1()
    gather_q[2].wave2()
    gather_q[1].wave2()

    def rotate(values_in):
        return values_in * cs[...] + pltpu.roll(values_in, HD // 2, 1) * sn[...]

    dq = dq_t[...].T
    for h in (0, 1):
        proj[c, :, pl.ds(h * HD, HD)] = rotate(dq[h * TOK : (h + 1) * TOK]).astype(BF)
    cross_q = remote(proj.at[c, :, pl.ds(0, QW)], proj.at[c, :, pl.ds(0, QW)], sib)
    cross_q.start()

    def pair_step(s, carry):
        cross_copy(s).wait_recv()
        ps[s] = (dkv[s, c].astype(F32) + sk[s].astype(F32)).astype(BF)
        return carry

    lax.fori_loop(0, CHIPS, pair_step, 0)
    send_d = [remote(ps.at[s], rk.at[back(s)], at(s // 4, s % 4)) for s in order]
    for copy in send_d:
        copy.start()

    scatter_o.a_near()
    for copy in load_x:
        copy.wait()
    for copy in cross_x:
        copy.wait_recv()
    cross_q.wait_recv()
    outer(1, proj[:, :, pl.ds(0, QW)].reshape(PAIR, QW).T, xi)
    scatter_q.begin()
    gather_q[3].wave2()
    scatter_o.b_far()

    for copy in frag_z:
        copy.wait_recv()
    home_z = pl.ds(pl.multiple_of(zh * 32, 32), 32)
    own = fs[home_z, :]
    for d in range(3):
        own = own + fzr[d].astype(F32)
    fs[home_z, :] = own
    frag_bz = [remote(fs.at[home_z], fs.at[home_z], dev) for dev in z_peers]
    for copy in frag_bz:
        copy.start()

    for copy in send_d:
        copy.wait_recv()

    def sum_step(s, carry):
        return carry + rk[s].astype(F32)

    kv = lax.fori_loop(1, CHIPS, sum_step, ps[0].astype(F32))
    proj[c, :, pl.ds(QW, HD)] = rotate(kv[:, :HD]).astype(BF)
    proj[c, :, pl.ds(QW + HD, HD)] = kv[:, HD:].astype(BF)
    cross_kv = remote(proj.at[c, :, pl.ds(QW, QW)], proj.at[c, :, pl.ds(QW, QW)], sib)
    cross_kv.start()
    cross_kv.wait_recv()
    outer(2, proj[:, :, pl.ds(QW, QW)].reshape(PAIR, QW).T, xi)
    scatter_k.begin()
    scatter_o.a_last()
    scatter_q.a_near()
    scatter_o.b_near()

    for copy in frag_bz:
        copy.wait_recv()
    home_x = pl.ds(pl.multiple_of(x * 128, 128), 128)
    for copy in frag_bz:
        copy.wait_send()
    fd[home_x, :] = fs[...]
    frag_bx = [remote(fs, fd.at[home_x], dev) for dev in x_peers]
    for copy in frag_bx:
        copy.start()

    scatter_k.a_near()
    scatter_q.b_far()

    for gather in gather_q:
        gather.finish()
    both = jnp.concatenate([proj[c], proj[o]], axis=0)
    cross_i = [remote(ig.at[s], input_out.at[0, :, columns(s, c)], sib) for s in range(CHIPS)]
    for s in range(CHIPS):
        block = dot_nt(both, wg[s, :, pl.ds(0, QKV)]).astype(BF)
        input_out[0, :, columns(s, c)] = block[:TOK]
        ig[s] = block[TOK:]
        cross_i[s].start()

    scatter_q.a_last()
    scatter_k.b_far()
    scatter_k.a_last()
    scatter_q.b_near()
    scatter_k.b_near()

    for copy in frag_bx:
        copy.wait_recv()
    for copy in load_t:
        copy.wait()
    outer_grad = fd[...] / replicas
    moment_next = outer_beta * fm[...] + outer_grad
    moment_out[...] = moment_next
    params_out[...] = fp[...] - outer_rate * (outer_grad + outer_beta * moment_next)

    scatter_o.end(QKV)
    scatter_q.end(0)
    scatter_k.end(QW)

    for copy in cross_i:
        copy.wait_recv()
    for copy in made:
        if not any(copy is other for other in frag_bz):
            copy.wait_send()

    def drain(s, carry):
        cross_copy(s).wait_send()
        return carry

    lax.fori_loop(0, CHIPS, drain, 0)


def body(inputs, out_grad, queries, key_states, value_states, weights, frag_delta, frag_params, frag_moment):
    anywhere = pl.BlockSpec(memory_space=pl.ANY)
    vm = pltpu.VMEM
    dma = pltpu.SemaphoreType.DMA
    return pl.pallas_call(
        functools.partial(kernel, float(lax.axis_size("replica"))),
        out_shape=(
            vm(inputs.shape, BF),
            vm(weights.shape, BF),
            vm(frag_params.shape, F32),
            vm(frag_moment.shape, F32),
        ),
        in_specs=[anywhere] * 9,
        out_specs=(pl.BlockSpec(memory_space=pltpu.VMEM),) * 4,
        scratch_shapes=[
            vm((CHIPS, 2, TOK, BLK), BF),
            vm((CHIPS, 2, TOK, BLK), BF),
            vm((CHIPS, BLK, WC), BF),
            vm((CHIPS, 2, TOK, HD), BF),
            vm((CHIPS, 2, TOK, HD), BF),
            vm((PAIR, HD), BF),
            vm((CHIPS, PAIR, PAIR), F32),
            vm((CHIPS, PAIR, PAIR), BF),
                vm((HD, PAIR), F32),
            vm((HD, PAIR), F32),
            vm((PAIR, HD), BF),
            vm((2, TOK, QW), F32),
            vm((TOK, QW), F32),
            vm((2, TOK, QW), BF),
            vm((2, TOK, QKV), BF),
            vm((CHIPS, 2, TOK, QW), BF),
            vm((CHIPS, TOK, QW), BF),
            vm((CHIPS, TOK, QW), BF),
            vm((CHIPS, TOK, QW), BF),
            vm((3, CHIPS, PART, BLK), BF),
            vm((3, YS, MOST_B, BLK), BF),
            vm((3, 2, MOST_A // 2, BLK), BF),
            vm((3, 2, MOST_A // 2, BLK), BF),
            vm((3, MOST_B // 2, BLK), BF),
            vm((3, MOST_B // 2, BLK), BF),
            vm((3, 2, PART, BLK), BF),
            vm((3, 2, MOST_A, BLK), BF),
            vm((3, MOST_A, BLK), BF),
            vm((CHIPS, TOK, BLK), BF),
            vm((TOK, HD), F32),
            vm((TOK, HD), F32),
            vm((512, 128), F32),
            vm((4, 128, 128), BF),
            vm((3, 128, 128), BF),
            vm((4, 32, 128), BF),
            vm((3, 32, 128), BF),
            vm((128, 128), F32),
            vm((512, 128), F32),
            vm((512, 128), F32),
            dma((64,)),
            dma((256,)),
            dma((256,)),
            dma((CHIPS,)),
            dma((CHIPS,)),
        ],
        compiler_params=pltpu.CompilerParams(
            collective_id=0, has_side_effects=True, vmem_limit_bytes=50 * 2**20
        ),
    )(inputs, out_grad, queries, key_states, value_states, weights, frag_delta, frag_params, frag_moment)


def solution(mesh):
    rows = P("replica", "fsdp", None)
    shared = P("fsdp", None)
    return jax.shard_map(
        body,
        mesh=mesh,
        in_specs=(rows,) * 7 + (shared,) * 2,
        out_specs=(rows, rows, shared, shared),
        check_vma=False,
    )
```

time: 135 us -> 117 us (0.87); the launches traced: 133 us -> 117 us
  Pallas kernels: 125 us -> 112 us
  local copies, waits for them, and re-layouts: 6.25 us -> 3.95 us
    pallas_call x1, Pallas kernels: 125 us -> 112 us  [body(): pl.pallas_call(functools.partial(kernel, float(lax.axis_size('replica')))...]
    unnamed x10 -> x4, local copies, waits for them, and re-layouts: 6.25 us -> 3.95 us
where the time goes in v2:
time: 117 us
  Pallas kernels  112 us (96%)
  local copies, waits for them, and re-layouts  3.95 us (3%)
    pallas_call x1, Pallas kernels, body(): pl.pallas_call(functools.partial(kernel, float(lax.axis_size('replica')))...  112 us
    unnamed x4, local copies, waits for them, and re-layouts  3.95 us

profile of v2, /device:TPU:1, one launch (start us, length us, event | category | flops | bytes accessed | tf_op | source)
XLA Modules:
  0.0 116.9 jit_solution(6968795285588497480)
XLA Ops:
  0.6 112.3 %shard_map.120 = (bf16[1,192,8192]{2,1,0:T(8,128)(2,1)S(1)}, bf16[1,512,768]{2,1,0:T(8,128)(2,1)S(1)}, f32[512,128]{1,0:T(8,128)S(1)}, f32[512,128]{1,0:T(8,128)S(1)}) custom-call(bf16[1,192,8192]{2,1,0:T(8,128)(2,1)} %inputs.1, bf16[1,192,8192]{2,1,0:T(8,128)(2,1)} %out_grad.1, bf16[1,192,256]{2,1,0:T(8,128)(2,1)} %queries.1, bf16[1,192,128]{2,1,0:T(8,128)(2,1)} %keys.1, ...), custom_call_target="tpu_custom_call" | custom-call | tf_op jit(solution)/shard_map/pallas_call | solution.py:626
  113.0 1.7 %copy.17 = bf16[1,192,8192]{2,1,0:T(8,128)(2,1)} copy(bf16[1,192,8192]{2,1,0:T(8,128)(2,1)S(1)} %get-tuple-element.4) | data formatting | bytes 6291456
  114.6 0.7 copy.19
  115.3 0.7 copy.20
  116.0 0.9 copy.18

commit v3 on v0

v3 whole, which is shorter than its diff:
```python
import functools
import math

import jax
import jax.numpy as jnp
from jax import lax
from jax.experimental import pallas as pl
from jax.experimental.pallas import tpu as pltpu
from jax.sharding import PartitionSpec as P

rope_base = 500000.0
outer_rate = 0.7
outer_beta = 0.9
masked_score = -1e30

BF = jnp.bfloat16
F32 = jnp.float32
MESH = pl.DeviceIdType.MESH

TOK = 192
PAIR = 2 * TOK
HD = 128
QW = 256
BLK = 512
WC = 768
QKV = 512
CHIPS = 8
YS = 4

WEIGHT_Z = 288
KEY_Z = 112
PARTS = (
    (192, 256, 112, 48, 48),
    (256, 512, 160, 80, 48),
    (256, 512, 128, 64, 64),
    (128, 512, 80, 48, 16),
    (128, 512, 80, 48, 16),
)
PART = 256
SEMS = 132

ORDER = (
    "K.w0", "V.w0", "o0.w0", "g.x", "f.x", "loads", "K.w1", "V.w1", "o1.w0", "V.w2", "K.w2",
    "o0.w1", "o1.w1", "kx", "vx", "q0.w0", "score", "o0.w2", "o1.w2", "q1.w0", "q2.w0", "value",
    "f.z", "q3.w0", "grad", "so.S", "q0.w1", "back", "q3.w1", "dq", "pair", "q1.w1", "so.b2", "d.S",
    "so.a3", "sq.S", "f.bz", "d.b2", "d.a3", "q1.w2", "so.b3", "d.b3", "d.a4", "q2.w1", "sq.a3",
    "kv", "q3.w2", "sk0.S", "q0.w2", "q2.w2", "sk1.S", "so.a4", "sk0.a3", "sq.b2", "f.bx", "sq.a4",
    "sk1.a3", "sk0.b2", "ig", "f.end", "sk1.b2", "sq.b3", "sk1.a4", "sk0.a4", "sk1.b3", "sk0.b3",
    "sq.fin", "so.fin", "sk1.fin", "sk0.fin",
)

NT = (((1,), (1,)), ((), ()))
TN = (((0,), (0,)), ((), ()))


def dot(a, b):
    return jnp.dot(a, b, preferred_element_type=F32)


def dot_nt(a, b):
    return lax.dot_general(a, b, NT, preferred_element_type=F32)


def dot_tn(a, b):
    return lax.dot_general(a, b, TN, preferred_element_type=F32)


def kernel(
    replicas,
    inputs,
    out_grad,
    queries,
    keys,
    values,
    weights,
    delta,
    params,
    moment,
    input_out,
    weight_out,
    params_out,
    moment_out,
    xi,
    xg,
    wg,
    kb,
    vb,
    qs,
    st,
    plow,
    att_t,
    dq_t,
    gs,
    agp,
    agr,
    att,
    proj,
    dkv,
    sk,
    ig,
    cs,
    sn,
    fd,
    fb,
    fr,
    fz,
    fzr,
    fs,
    fp,
    fm,
    sems,
    *parts,
):
    r = lax.axis_index("replica")
    f = lax.axis_index("fsdp")
    c = lax.rem(f, 2)
    y = lax.rem(f // 2, YS)
    z = f // (2 * YS)
    o = 1 - c
    x = lax.rem(r, 4)
    zh = r // 4

    def chip(dz, dy):
        return lax.rem(z + dz, 2) * YS + lax.rem(y + dy, YS)

    def at(dz, dy, core=None):
        return (r, chip(dz, dy) * 2 + (c if core is None else core))

    yp, ym, zp, sib = at(0, 1), at(0, 3), at(1, 0), at(0, 0, o)

    def back(s):
        return (s // 4) * 4 + (4 - s % 4) % 4

    taken = []

    def sem():
        taken.append(1)
        return sems.at[len(taken) - 1]

    def remote(src, dst, dev, sent, landed):
        return pltpu.make_async_remote_copy(
            src_ref=src,
            dst_ref=dst,
            send_sem=sent,
            recv_sem=landed,
            device_id=dev,
            device_id_type=MESH,
        )

    class Load:
        def __init__(self, whole, pairs):
            self.whole, self.sem = whole, sem()
            for src, dst in pairs:
                pltpu.make_async_copy(src, dst, self.sem).start()

        def wait(self):
            pltpu.make_async_copy(self.whole, self.whole, self.sem).wait()

    class Cross:
        def __init__(self, whole, triples):
            self.sent, self.landed = sem(), sem()
            self.all = remote(whole, whole, sib, self.sent, self.landed)
            self.copies = [remote(src, dst, dev, self.sent, self.landed) for src, dst, dev in triples]

        def start(self):
            for copy in self.copies:
                copy.start()

        def wait_recv(self):
            self.all.wait_recv()

        def wait_send(self):
            self.all.wait_send()

    def slot_chip(s):
        return lax.rem(z + s // 4, 2) * YS + lax.rem(y + s % 4, YS)

    def columns(s, core):
        return pl.ds(pl.multiple_of((slot_chip(s) * 2 + core) * BLK, BLK), BLK)

    load_q = Load(qs, [(queries.at[0, :, pl.ds(h * HD, HD)], qs.at[pl.ds(h * TOK, TOK)]) for h in (0, 1)])
    load_k = Load(kb.at[0, c], [(keys.at[0], kb.at[0, c])])
    load_v = Load(vb.at[0, c], [(values.at[0], vb.at[0, c])])
    load_w = Load(wg.at[0], [(weights.at[0], wg.at[0])])
    load_d = Load(fd, [(delta.at[0], fd)])
    load_g = Load(xg.at[:, c], [(out_grad.at[0, :, columns(s, c)], xg.at[s, c]) for s in range(CHIPS)])
    load_x = Load(xi.at[:, c], [(inputs.at[0, :, columns(s, c)], xi.at[s, c]) for s in range(CHIPS)])
    load_p = Load(fp, [(params, fp)])
    load_m = Load(fm, [(moment, fm)])

    peers = [yp, ym, zp, sib]
    x_peers = [(zh * 4 + lax.rem(x + d, 4), f) for d in (1, 2, 3)]
    z_peers = [(lax.rem(zh + d, 4) * 4 + x, f) for d in (1, 2, 3)]
    barrier = pltpu.get_barrier_semaphore()
    for dev in peers + x_peers + z_peers:
        pl.semaphore_signal(barrier, inc=1, device_id=dev, device_id_type=MESH)
    pos = (f * TOK + lax.broadcasted_iota(jnp.int32, (TOK, HD), 0)).astype(F32)
    lane = lax.broadcasted_iota(jnp.int32, (1, HD), 1)
    step_of = jnp.where(lane >= HD // 2, lane - HD // 2, lane).astype(F32)
    angles = pos * jnp.exp(-math.log(rope_base) * 2.0 * step_of / HD)
    cs[...] = jnp.cos(angles)
    sine = jnp.sin(angles)
    sn[...] = jnp.where(lane >= HD // 2, -sine, sine)
    pl.semaphore_wait(barrier, len(peers) + 6)

    class Gather:
        def __init__(self, own, rows, extent, first, sent, rest, two, near):
            def move(src, dst, lo, hi, dev, landed):
                return remote(rows(src, lo, hi), rows(dst, lo, hi), dev, sent, landed)

            half = first // 32 * 16
            self.s3 = remote(own, rows(3, 0, extent), yp, sent, sem())
            self.s1 = remote(own, rows(1, 0, extent), ym, sent, sem())
            self.s4 = remote(own, rows(4, 0, extent), zp, sent, sem())
            far, close = sem(), sem()
            self.s2a = move(1, 2, 0, extent // 2, ym, far)
            self.s2b = move(3, 2, extent // 2, extent, yp, far)
            self.s7a = move(4, 7, 0, first, yp, close)
            self.s5a = move(4, 5, 0, first, ym, close)
            self.s5b = move(1, 5, first, extent, zp, rest)
            self.s7b = move(3, 7, first, extent, zp, rest)
            self.s6b = move(2, 6, first, extent, zp, rest)
            self.s6a1 = move(5, 6, 0, half, ym, rest)
            self.s6a2 = move(7, 6, half, first, yp, rest)
            self.two = remote(two, two, sib, sent, far)
            self.near = remote(near, near, sib, sent, close)

        def wave0(self):
            self.s3.start()
            self.s1.start()
            self.s4.start()

        def wave1(self):
            self.s1.wait_recv()
            self.s2a.start()
            self.s5b.start()
            self.s3.wait_recv()
            self.s2b.start()
            self.s7b.start()
            self.s4.wait_recv()
            self.s7a.start()
            self.s5a.start()

        def wave2(self):
            self.two.wait_recv()
            self.s6b.start()
            self.near.wait_recv()
            self.s6a1.start()
            self.s6a2.start()

    def gather_states(source, target):
        sent, rest = sem(), sem()
        gather = Gather(
            source.at[0],
            lambda s, lo, hi: target.at[s, c, pl.ds(lo, hi - lo)],
            TOK,
            KEY_Z,
            sent,
            rest,
            target.at[0, c],
            qs.at[pl.ds(0, 2 * KEY_Z)],
        )
        left = qs.at[pl.ds(0, 3 * (TOK - KEY_Z) + KEY_Z)]
        every = target.at[pl.ds(0, CHIPS - 1), c]
        return gather, remote(every, left, sib, sent, rest)

    sent_w, rest_o, rest_q = sem(), sem(), sem()

    def gather_weights(first, rest):
        cols = pl.ds(first, HD)
        return Gather(
            weights.at[0, :, cols],
            lambda s, lo, hi: wg.at[s, pl.ds(lo, hi - lo), cols],
            BLK,
            WEIGHT_Z,
            sent_w,
            rest,
            wg.at[0, :, cols],
            wg.at[0, pl.ds(0, 2 * WEIGHT_Z * HD // WC), :],
        )

    def left_of(pieces):
        rows = pieces * (3 * (BLK - WEIGHT_Z) + WEIGHT_Z) * HD // WC // 5
        return wg.at[pl.ds(0, 5), pl.ds(0, rows), :]

    gather_key, all_key = gather_states(keys, kb)
    gather_value, all_value = gather_states(values, vb)
    gather_o = [gather_weights(QKV + HD * i, rest_o) for i in range(2)]
    gather_q = [gather_weights(HD * i, rest_q) for i in range(4)]
    all_o = remote(wg.at[pl.ds(0, CHIPS - 1)], left_of(2), sib, sent_w, rest_o)
    all_q = remote(wg.at[pl.ds(0, CHIPS - 1)], left_of(4), sib, sent_w, rest_q)
    cross_k = Cross(
        kb.at[:, c], [(keys.at[0] if s == 0 else kb.at[s, c], kb.at[s, c], sib) for s in range(CHIPS)]
    )
    cross_v = Cross(
        vb.at[:, c], [(values.at[0] if s == 0 else vb.at[s, c], vb.at[s, c], sib) for s in range(CHIPS)]
    )

    cross_g = Cross(
        xg.at[:, c], [(out_grad.at[0, :, columns(s, o)], xg.at[s, c], sib) for s in range(CHIPS)]
    )
    cross_x = Cross(
        xi.at[:, c], [(inputs.at[0, :, columns(s, o)], xi.at[s, c], sib) for s in range(CHIPS)]
    )
    half_q, half_kv = proj.at[c, :, pl.ds(0, QW)], proj.at[c, :, pl.ds(QW, QW)]
    cross_a = Cross(att.at[c], [(att.at[c], att.at[c], sib)])
    cross_p = Cross(agr, [(agp.at[o], agr, sib)])
    cross_q = Cross(half_q, [(half_q, half_q, sib)])
    cross_kv = Cross(half_kv, [(half_kv, half_kv, sib)])
    cross_i = Cross(ig, [(ig.at[s], input_out.at[0, :, columns(s, c)], sib) for s in range(CHIPS)])
    sent_d, landed_d = sem(), sem()
    cross_d = remote(sk, sk, sib, sent_d, landed_d)

    home_x = pl.ds(pl.multiple_of(x * 128, 128), 128)
    home_z = pl.ds(pl.multiple_of(zh * 32, 32), 32)
    frag_x = Cross(fr, [(fb.at[lax.rem(x + d, 4)], fr.at[d - 1], x_peers[d - 1]) for d in (1, 2, 3)])
    frag_z = Cross(fzr, [(fz.at[lax.rem(zh + d, 4)], fzr.at[d - 1], z_peers[d - 1]) for d in (1, 2, 3)])
    frag_bz = Cross(fs.at[pl.ds(0, 96)], [(fs.at[home_z], fs.at[home_z], dev) for dev in z_peers])
    frag_bx = Cross(fd.at[pl.ds(0, 384)], [(fs, fd.at[home_x], dev) for dev in x_peers])

    def fragment_start():
        load_d.wait()
        for j in range(4):
            fb[j] = fd[pl.ds(j * 128, 128), :].astype(BF)
        frag_x.start()

    def fragment_over_z():
        frag_x.wait_recv()
        partial = fd[home_x, :]
        for d in range(3):
            partial = partial + fr[d].astype(F32)
        fs[...] = partial
        fz[...] = partial.astype(BF).reshape(4, 32, 128)
        frag_z.start()

    def fragment_back_z():
        frag_z.wait_recv()
        own = fs[home_z, :]
        for d in range(3):
            own = own + fzr[d].astype(F32)
        fs[home_z, :] = own
        frag_bz.start()

    def fragment_back_x():
        frag_bz.wait_recv()
        frag_bz.wait_send()
        fd[home_x, :] = fs[...]
        frag_bx.start()

    def fragment_end():
        frag_bx.wait_recv()
        load_p.wait()
        load_m.wait()
        outer_grad = fd[...] / replicas
        moment_next = outer_beta * fm[...] + outer_grad
        moment_out[...] = moment_next
        params_out[...] = fp[...] - outer_rate * (outer_grad + outer_beta * moment_next)

    held = {}
    scale = 1.0 / math.sqrt(HD)

    class Scatter:
        def __init__(self, n):
            part, rzp, up, down, bup, bdown, near, cross, final = parts[9 * n : 9 * n + 9]
            extent, _, a, a1, half = PARTS[n]
            self.part, self.a, self.a1, self.b1, self.extent = part, a, a1, a + half, extent
            self.rz, self.up, self.down, self.bup, self.bdown = rzp, up, down, bup, bdown
            self.near, self.cross, self.final = near, cross, final
            far = tuple(enumerate((2, 6)))
            top, rest = pl.ds(0, a), pl.ds(a, extent - a)
            sent = sem()
            self.sent = remote(part.at[pl.ds(0, CHIPS - 1)], part.at[0], sib, sent, sent)
            self.to_z = remote(part.at[pl.ds(4, 4), rest], rzp, zp, sent, sem())
            landed = sem()
            self.a_up = [remote(part.at[s, pl.ds(0, a1)], up.at[i], yp, sent, landed) for i, s in far]
            self.up_all = remote(up, up, sib, sent, landed)
            landed = sem()
            self.a_down = [
                remote(part.at[s, pl.ds(a1, a - a1)], down.at[i], ym, sent, landed) for i, s in far
            ]
            self.down_all = remote(down, down, sib, sent, landed)
            self.b_up = remote(part.at[2, pl.ds(a, half)], bup, yp, sent, sem())
            self.b_down = remote(part.at[2, pl.ds(a + half, extent - a - half)], bdown, ym, sent, sem())
            landed = sem()
            self.g = [
                remote(part.at[5, top], cross.at[0], yp, sent, landed),
                remote(part.at[7, top], cross.at[1], ym, sent, landed),
            ]
            self.g_all = remote(cross, cross, sib, sent, landed)
            landed = sem()
            self.fa = [
                remote(part.at[1, top], near.at[0, top], yp, sent, landed),
                remote(part.at[3, top], near.at[1, top], ym, sent, landed),
            ]
            self.fb = [
                remote(part.at[1, rest], near.at[0, rest], yp, sent, landed),
                remote(part.at[3, rest], near.at[1, rest], ym, sent, landed),
            ]
            self.f_all = remote(near, near, sib, sent, landed)
            self.last = remote(part.at[4, top], final, zp, sent, sem())

        def add(self, s, lo, hi, *others):
            rows = pl.ds(lo, hi - lo)
            value = self.part[s, rows, :].astype(F32)
            for other in others:
                value = value + other[...].astype(F32)
            self.part[s, rows, :] = value.astype(BF)

        def begin(self):
            for copy in self.a_up + self.a_down:
                copy.start()
            self.to_z.start()

        def a_near(self):
            a, a1 = self.a, self.a1
            self.up_all.wait_recv()
            self.add(5, 0, a1, self.up.at[1])
            self.g[0].start()
            self.add(1, 0, a1, self.up.at[0])
            self.fa[0].start()
            self.down_all.wait_recv()
            self.add(7, a1, a, self.down.at[1])
            self.g[1].start()
            self.add(3, a1, a, self.down.at[0])
            self.fa[1].start()

        def a_last(self):
            self.g_all.wait_recv()
            self.add(4, 0, self.a, self.cross.at[0], self.cross.at[1])
            self.last.start()

        def b_far(self):
            a, extent = self.a, self.extent
            self.to_z.wait_recv()
            self.add(2, a, extent, self.rz.at[2])
            self.b_up.start()
            self.b_down.start()
            for s in (1, 3, 0):
                self.add(s, a, extent, self.rz.at[s])

        def b_near(self):
            a, b1 = self.a, self.b1
            self.b_up.wait_recv()
            self.add(1, a, b1, self.bup)
            self.fb[0].start()
            self.b_down.wait_recv()
            self.add(3, b1, self.extent, self.bdown)
            self.fb[1].start()

        def total(self):
            a = self.a
            self.f_all.wait_recv()
            self.last.wait_recv()
            value = self.part[0].astype(F32) + self.near[0].astype(F32) + self.near[1].astype(F32)
            top = value[:a] + self.final[...].astype(F32)
            return jnp.concatenate([top, value[a:]], axis=0)

    def finish_part(scatter, first):
        weight_out[0, :, pl.ds(first, scatter.extent)] = scatter.total().T.astype(BF)

    scatter_d, scatter_o, scatter_q, scatter_k, scatter_v = [Scatter(n) for n in range(5)]

    def outer(scatter, left, right):
        def step(s, carry):
            scatter.part[s] = dot(left, right[s].reshape(PAIR, BLK)).astype(BF)
            return carry

        lax.fori_loop(0, CHIPS, step, 0)

    def first_loads():
        load_k.wait()
        load_v.wait()
        load_w.wait()

    def cross_keys():
        all_key.wait_recv()
        cross_k.start()

    def cross_values():
        all_value.wait_recv()
        cross_v.start()
        cross_x.start()

    def score_step(s, peak):
        part = dot_nt(kb[s].reshape(PAIR, HD), qs[...]) * scale
        key_pos = slot_chip(s) * PAIR + lax.broadcasted_iota(jnp.int32, (PAIR, PAIR), 0)
        lane = lax.broadcasted_iota(jnp.int32, (1, PAIR), 1)
        query_pos = f * TOK + jnp.where(lane >= TOK, lane - TOK, lane)
        part = jnp.where(key_pos <= query_pos, part, masked_score)
        st[s] = part
        return jnp.maximum(peak, jnp.max(part, axis=0, keepdims=True))

    def score():
        load_q.wait()
        cross_k.wait_recv()
        peak = lax.fori_loop(0, CHIPS, score_step, jnp.full((1, PAIR), masked_score, F32))

        def exp_step(s, total):
            part = jnp.exp(st[s] - peak)
            st[s] = part
            return total + jnp.sum(part, axis=0, keepdims=True)

        total = lax.fori_loop(0, CHIPS, exp_step, jnp.zeros((1, PAIR), F32))
        held["inverse"] = 1.0 / total

    def value():
        cross_v.wait_recv()
        att_t[...] = jnp.zeros_like(att_t)
        inverse = held["inverse"]

        def value_step(s, carry):
            part = st[s] * inverse
            st[s] = part
            low = part.astype(BF)
            plow[s] = low
            att_t[...] += dot_tn(vb[s].reshape(PAIR, HD), low)
            return carry

        lax.fori_loop(0, CHIPS, value_step, 0)
        attended = att_t[...].T.astype(BF)
        for h in (0, 1):
            att[c, :, pl.ds(h * HD, HD)] = attended[h * TOK : (h + 1) * TOK]
        cross_a.start()

    def grad():
        load_g.wait()
        cross_g.wait_recv()
        all_o.wait_recv()
        agp[...] = jnp.zeros_like(agp)

        def grad_step(s, carry):
            part = dot(xg[s].reshape(PAIR, BLK), wg[s, :, pl.ds(QKV, QW)])
            agp[...] += part.reshape(2, TOK, QW)
            return carry

        lax.fori_loop(0, CHIPS, grad_step, 0)
        cross_p.start()

    def back_all():
        cross_p.wait_recv()
        own = (agp[c] + agr[...]).astype(BF)
        for h in (0, 1):
            gs[pl.ds(h * TOK, TOK), :] = own[:, h * HD : (h + 1) * HD]
        row_delta = jnp.sum(att_t[...] * gs[...].astype(F32).T, axis=0, keepdims=True)
        dq_t[...] = jnp.zeros_like(dq_t)

        def back_step(s, carry):
            prob_grad = dot_nt(vb[s].reshape(PAIR, HD), gs[...])
            low = (st[s] * (prob_grad - row_delta) * scale).astype(BF)
            dq_t[...] += dot_tn(kb[s].reshape(PAIR, HD), low)
            dkv[s, :, :, pl.ds(0, HD)] = dot(low, qs[...]).astype(BF).reshape(2, TOK, HD)
            dkv[s, :, :, pl.ds(HD, HD)] = dot(plow[s], gs[...]).astype(BF).reshape(2, TOK, HD)
            remote(dkv.at[s, o], sk.at[s], sib, sent_d, landed_d).start()
            return carry

        lax.fori_loop(0, CHIPS, back_step, 0)

    def rotate(values_in):
        return values_in * cs[...] + pltpu.roll(values_in, HD // 2, 1) * sn[...]

    def query_grad():
        dq = dq_t[...].T
        for h in (0, 1):
            proj[c, :, pl.ds(h * HD, HD)] = rotate(dq[h * TOK : (h + 1) * TOK]).astype(BF)
        cross_q.start()

    def pair():
        cross_d.wait_recv()

        def pair_step(s, carry):
            scatter_d.part[s] = (dkv[s, c].astype(F32) + sk[s].astype(F32)).astype(BF)
            return carry

        lax.fori_loop(0, CHIPS, pair_step, 0)

    def key_value_grad():
        kv = scatter_d.total()
        proj[c, :, pl.ds(QW, HD)] = rotate(kv[:, :HD]).astype(BF)
        proj[c, :, pl.ds(QW + HD, HD)] = kv[:, HD:].astype(BF)
        cross_kv.start()

    def out_begin():
        cross_a.wait_recv()
        outer(scatter_o, att[...].reshape(PAIR, QW).T, xg)
        scatter_o.begin()

    def query_begin():
        load_x.wait()
        cross_x.wait_recv()
        cross_q.wait_recv()
        outer(scatter_q, proj[:, :, pl.ds(0, QW)].reshape(PAIR, QW).T, xi)
        scatter_q.begin()

    def key_begin():
        cross_kv.wait_recv()
        outer(scatter_k, proj[:, :, pl.ds(QW, HD)].reshape(PAIR, HD).T, xi)
        scatter_k.begin()

    def value_begin():
        outer(scatter_v, proj[:, :, pl.ds(QW + HD, HD)].reshape(PAIR, HD).T, xi)
        scatter_v.begin()

    def inputs_grad():
        all_q.wait_recv()
        both = jnp.concatenate([proj[c], proj[o]], axis=0)
        for s in range(CHIPS):
            block = dot_nt(both, wg[s, :, pl.ds(0, QKV)]).astype(BF)
            input_out[0, :, columns(s, c)] = block[:TOK]
            ig[s] = block[TOK:]
            cross_i.copies[s].start()

    tasks = {
        "loads": first_loads,
        "g.x": cross_g.start,
        "kx": cross_keys,
        "vx": cross_values,
        "score": score,
        "value": value,
        "grad": grad,
        "back": back_all,
        "dq": query_grad,
        "pair": pair,
        "kv": key_value_grad,
        "ig": inputs_grad,
        "f.x": fragment_start,
        "f.z": fragment_over_z,
        "f.bz": fragment_back_z,
        "f.bx": fragment_back_x,
        "f.end": fragment_end,
        "so.S": out_begin,
        "sq.S": query_begin,
        "sk0.S": key_begin,
        "sk1.S": value_begin,
        "d.S": scatter_d.begin,
    }
    gathers = {"K": gather_key, "V": gather_value}
    gathers.update({"o%d" % i: gather for i, gather in enumerate(gather_o)})
    gathers.update({"q%d" % i: gather for i, gather in enumerate(gather_q)})
    for name, gather in gathers.items():
        tasks.update({name + ".w0": gather.wave0, name + ".w1": gather.wave1, name + ".w2": gather.wave2})
    ends = (("d", scatter_d, None), ("so", scatter_o, QKV), ("sq", scatter_q, 0))
    for name, scatter, first in ends + (("sk0", scatter_k, QW), ("sk1", scatter_v, QW + HD)):
        tasks.update({name + ".a3": scatter.a_near, name + ".a4": scatter.a_last})
        tasks.update({name + ".b2": scatter.b_far, name + ".b3": scatter.b_near})
        tasks[name + ".fin"] = functools.partial(finish_part, scatter, first)
    for name in ORDER:
        tasks[name]()

    cross_i.wait_recv()
    for group in (cross_k, cross_v, cross_g, cross_x, cross_a, cross_p, cross_q, cross_kv, cross_i):
        group.wait_send()
    for group in (frag_x, frag_z, frag_bx, all_key, all_value, all_o, cross_d):
        group.wait_send()
    for scatter in (scatter_o, scatter_q, scatter_k, scatter_v, scatter_d):
        scatter.sent.wait_send()
    assert len(taken) <= SEMS


def part_buffers(rows, cols, a, a1, half):
    b = rows - a
    shapes = (
        (CHIPS, rows, cols),
        (YS, b, cols),
        (2, a1, cols),
        (2, a - a1, cols),
        (half, cols),
        (b - half, cols),
        (2, rows, cols),
        (2, a, cols),
        (a, cols),
    )
    return [pltpu.VMEM(shape, BF) for shape in shapes]


def store(*refs):
    sems = refs[8]
    copies = [pltpu.make_async_copy(refs[i], refs[4 + i], sems.at[i]) for i in range(4)]
    for copy in copies:
        copy.start()
    for copy in copies:
        copy.wait()


def body(inputs, out_grad, queries, key_states, value_states, weights, frag_delta, frag_params, frag_moment):
    anywhere = pl.BlockSpec(memory_space=pl.ANY)
    vm = pltpu.VMEM
    dma = pltpu.SemaphoreType.DMA
    results = pl.pallas_call(
        functools.partial(kernel, float(lax.axis_size("replica"))),
        out_shape=(
            vm(inputs.shape, BF),
            vm(weights.shape, BF),
            vm(frag_params.shape, F32),
            vm(frag_moment.shape, F32),
        ),
        in_specs=[anywhere] * 9,
        out_specs=(pl.BlockSpec(memory_space=pltpu.VMEM),) * 4,
        scratch_shapes=[
            vm((CHIPS, 2, TOK, BLK), BF),
            vm((CHIPS, 2, TOK, BLK), BF),
            vm((CHIPS, BLK, WC), BF),
            vm((CHIPS, 2, TOK, HD), BF),
            vm((CHIPS, 2, TOK, HD), BF),
            vm((PAIR, HD), BF),
            vm((CHIPS, PAIR, PAIR), F32),
            vm((CHIPS, PAIR, PAIR), BF),
                vm((HD, PAIR), F32),
            vm((HD, PAIR), F32),
            vm((PAIR, HD), BF),
            vm((2, TOK, QW), F32),
            vm((TOK, QW), F32),
            vm((2, TOK, QW), BF),
            vm((2, TOK, QKV), BF),
            vm((CHIPS, 2, TOK, QW), BF),
            vm((CHIPS, TOK, QW), BF),
            vm((CHIPS, TOK, BLK), BF),
            vm((TOK, HD), F32),
            vm((TOK, HD), F32),
            vm((512, 128), F32),
            vm((4, 128, 128), BF),
            vm((3, 128, 128), BF),
            vm((4, 32, 128), BF),
            vm((3, 32, 128), BF),
            vm((128, 128), F32),
            vm((512, 128), F32),
            vm((512, 128), F32),
            dma((SEMS,)),
        ]
        + [shape for part in PARTS for shape in part_buffers(*part)],
        compiler_params=pltpu.CompilerParams(
            collective_id=0, has_side_effects=True, vmem_limit_bytes=58 * 2**20
        ),
    )(inputs, out_grad, queries, key_states, value_states, weights, frag_delta, frag_params, frag_moment)
    return pl.pallas_call(
        store,
        out_shape=[jax.ShapeDtypeStruct(value.shape, value.dtype) for value in results],
        in_specs=[pl.BlockSpec(memory_space=pl.ANY)] * 4,
        out_specs=[pl.BlockSpec(memory_space=pl.ANY)] * 4,
        scratch_shapes=[dma((4,))],
        compiler_params=pltpu.CompilerParams(vmem_limit_bytes=2**20),
    )(*[pltpu.with_memory_space_constraint(value, pltpu.VMEM) for value in results])


def solution(mesh):
    rows = P("replica", "fsdp", None)
    shared = P("fsdp", None)
    return jax.shard_map(
        body,
        mesh=mesh,
        in_specs=(rows,) * 7 + (shared,) * 2,
        out_specs=(rows, rows, shared, shared),
        check_vma=False,
    )
```

time: 345 us -> 107 us (0.31)
  waiting for transfers between devices: 206 us -> 0 us
  Pallas kernels: 0 us -> 106 us
  blocking collectives: 51.8 us -> 0 us
  matrix products: 51.3 us -> 0 us
  between operations: 15.4 us -> 0.64 us
  other arithmetic: 14.4 us -> 0 us
    reduce_scatter x3 -> x0, waiting for transfers between devices: 158 us -> none  [the longest x1 64.2 us: body(): lax.psum_scatter(value_term.astype(jnp.bfloat16), 'fsdp', scatter_dimensi...]
    pallas_call x0 -> x2, Pallas kernels: none -> 106 us  [the longest x1 104 us: body(): pl.pallas_call(functools.partial(kernel, float(lax.axis_size('replica')))...]
    all_gather x2 -> x0, blocking collectives: 51.8 us -> none  [the longest x1 27.2 us: body(): lax.all_gather(key_states[0], 'fsdp', axis=0, tiled=True)]
    dot_general x9 -> x0, matrix products: 46 us -> none  [the longest x1 8.69 us: body(): jnp.einsum('htk,thd->kd', score_grad, own_queries, preferred_element_type...]
    all_gather x1 -> x0, waiting for transfers between devices: 24.4 us -> none  [body(): full_weights = lax.all_gather(weights[0], 'fsdp', axis=0, tiled=True)]
    psum x1 -> x0, waiting for transfers between devices: 22.3 us -> none  [body(): lax.psum(frag_delta[0].astype(jnp.bfloat16), 'replica').astype(jnp.float32)]
    concatenate x1 -> x0, other arithmetic: 8.59 us -> none  [body(): jnp.concatenate([qkv_term, out_term], axis=1).astype(jnp.bfloat16)]
    sub x1 -> x0, matrix products: 5.3 us -> none  [body(): exponent = jnp.exp(scores - row_peak)]
  transfers between devices with their start and end apart: 5 -> 0, of which waited for: 5 -> 0; matrix products, arithmetic and copies ran while one was open for 15% -> 0% of each run, Pallas kernels for 0% -> 0%
where the time goes in v3:
time: 107 us; the launch traced here: 106 us
  Pallas kernels  106 us (99%)
    pallas_call x1, Pallas kernels, body(): pl.pallas_call(functools.partial(kernel, float(lax.axis_size('replica')))...  104 us

profile of v3, /device:TPU:1, one launch (start us, length us, event | category | flops | bytes accessed | tf_op | source)
XLA Modules:
  0.0 106.4 jit_solution(6388175200425474926)
XLA Ops:
  0.6 103.7 %shard_map.120 = (bf16[1,192,8192]{2,1,0:T(8,128)(2,1)S(1)}, bf16[1,512,768]{2,1,0:T(8,128)(2,1)S(1)}, f32[512,128]{1,0:T(8,128)S(1)}, f32[512,128]{1,0:T(8,128)S(1)}) custom-call(bf16[1,192,8192]{2,1,0:T(8,128)(2,1)} %inputs.1, bf16[1,192,8192]{2,1,0:T(8,128)(2,1)} %out_grad.1, bf16[1,192,256]{2,1,0:T(8,128)(2,1)} %queries.1, bf16[1,192,128]{2,1,0:T(8,128)(2,1)} %keys.1, ...), custom_call_target="tpu_custom_call" | custom-call | tf_op jit(solution)/shard_map/pallas_call | solution.py:688
  104.3 2.1 %shard_map.121 = (bf16[1,192,8192]{2,1,0:T(8,128)(2,1)}, bf16[1,512,768]{2,1,0:T(8,128)(2,1)}, f32[512,128]{1,0:T(8,128)}, f32[512,128]{1,0:T(8,128)}) custom-call(bf16[1,192,8192]{2,1,0:T(8,128)(2,1)S(1)} %get-tuple-element.8.refs_0_, bf16[1,512,768]{2,1,0:T(8,128)(2,1)S(1)} %get-tuple-element.9.refs_1_, f32[512,128]{1,0:T(8,128)S(1)} %get-tuple-element.10.refs_2_, ...), custom_call_target="tpu_custom_call" | custom-call | tf_op jit(solution)/shard_map/pallas_call | solution.py:734
